TPU v7x, 32 devices: a whole 2x2x4 slice. The times are simulated.
32 devices in a mesh: layer: 4 (over x, core), sph: 8 (over z, y).
Axes of the slice: x: 2, y: 2, z: 4, core: 2. Of those that a mesh axis runs over, the one named last changes fastest.
Arguments:
- out_basis: float32 [4, 2, 2, 48, 512], P('layer'), may hold values from -0.875 to 0.875
- in_basis: float32 [4, 2, 48, 512], P('layer'), may hold values from -0.875 to 0.875
- tmatrix: float32 [4, 128, 2, 48, 48], P('layer', 'sph'), may hold values from -0.0078125 to 0.0078125
- sites: int32 [4, 128], P('layer', 'sph'), may hold values from 0 to 1023
- waves: int32 [2, 256], replicated, may hold values from -12 to 12
- layer_phase: float32 [4, 512], P('layer'), may hold values from -3.140625 to 3.140625
Outputs:
- film_reflection: float32 [2, 512, 512], P(None, 'sph', 'layer')
- film_transmission: float32 [2, 512, 512], P(None, 'sph', 'layer')
All inputs are finite; a program needn't handle non-finite values.
Results may differ from a plain program's by a relative error of at most 0.025.
Values may be sent and summed in bfloat16 or wider, within the bound.
No kernel may reach another device: no remote copies, remote signals or barrier semaphores. Data moves between devices by JAX's collectives and lax.ppermute only.
A program may use at most 64 MiB of HBM per device.

v0:
```python
import functools
import math

import jax
import jax.numpy as jnp
from jax import lax
from jax.experimental import pallas as pl
from jax.experimental.pallas import tpu as pltpu
from jax.sharding import PartitionSpec as P

LATTICE = 32
TWO_PI = 2.0 * math.pi
F32 = jnp.float32
BF16 = jnp.bfloat16
VMEM = pl.BlockSpec(memory_space=pltpu.VMEM)
ANY = pl.BlockSpec(memory_space=pl.ANY)
SMEM = pl.BlockSpec(memory_space=pltpu.SMEM)
EXTRA = 16


def partner_2(value, axis, bit):
    mask = 2**bit
    pairs = [(source, source ^ mask) for source in range(lax.axis_size(axis))]
    return lax.ppermute(value, axis, pairs)


def wave_angles(site_list, waves):
    column = site_list // LATTICE
    along = site_list % LATTICE
    phase_index = (
        waves[0][None, :] * column[:, None] + waves[1][None, :] * along[:, None]
    ) % LATTICE
    angles = phase_index.astype(jnp.float32) * (TWO_PI / LATTICE)
    return jnp.concatenate([angles, angles], axis=1)


def factors(out_layer, in_layer, tm_layer, angles):
    highest = lax.Precision.HIGHEST
    basis_re = out_layer[:, 0]
    basis_im = out_layer[:, 1]
    tmat_re = tm_layer[:, 0]
    tmat_im = tm_layer[:, 1]
    prod_re = jnp.einsum("kjw,sjm->ksmw", basis_re, tmat_re, precision=highest) - jnp.einsum(
        "kjw,sjm->ksmw", basis_im, tmat_im, precision=highest
    )
    prod_im = jnp.einsum("kjw,sjm->ksmw", basis_re, tmat_im, precision=highest) + jnp.einsum(
        "kjw,sjm->ksmw", basis_im, tmat_re, precision=highest
    )
    cosine = jnp.cos(angles)
    sine = jnp.sin(angles)
    left_re = prod_re * cosine[None, :, None, :] - prod_im * sine[None, :, None, :]
    left_im = prod_re * sine[None, :, None, :] + prod_im * cosine[None, :, None, :]
    right_re = in_layer[0][None] * cosine[:, None, :] + in_layer[1][None] * sine[:, None, :]
    right_im = in_layer[1][None] * cosine[:, None, :] - in_layer[0][None] * sine[:, None, :]
    inner = left_re.shape[1] * left_re.shape[2]
    width = left_re.shape[3]
    left_re = left_re.reshape(2, inner, width)
    left_im = left_im.reshape(2, inner, width)
    right_re = right_re.reshape(inner, width)
    right_im = right_im.reshape(inner, width)
    real_left = jnp.concatenate([left_re, -left_im], axis=1)
    imag_left = jnp.concatenate([left_re, left_im], axis=1)
    real_right = jnp.concatenate([right_re, right_im], axis=0)
    imag_right = jnp.concatenate([right_im, right_re], axis=0)
    return (real_left, imag_left, real_right, imag_right)


def project_rows(factor_set):
    real_left, imag_left, real_right, imag_right = factor_set
    highest = lax.Precision.HIGHEST
    pieces = []
    for kind in range(2):
        real_slice = real_left[kind]
        imag_slice = imag_left[kind]
        pieces.append(jnp.einsum("kr,kw->rw", real_slice, real_right, precision=highest))
        pieces.append(jnp.einsum("kr,kw->rw", imag_slice, imag_right, precision=highest))
    return jnp.concatenate(pieces, axis=1)


def narrow(matrix):
    return matrix.astype(jnp.bfloat16)


def complex_product(left, right):
    left_half = narrow(left)
    right_half = narrow(right)
    real_part = jnp.dot(left_half[0], right_half[0], preferred_element_type=jnp.float32) - jnp.dot(
        left_half[1], right_half[1], preferred_element_type=jnp.float32
    )
    imag_part = jnp.dot(left_half[0], right_half[1], preferred_element_type=jnp.float32) + jnp.dot(
        left_half[1], right_half[0], preferred_element_type=jnp.float32
    )
    return jnp.stack([real_part, imag_part])


def merge_level(state, bit):
    partner = partner_2(state.astype(jnp.bfloat16), "layer", bit).astype(state.dtype)
    is_upper = lax.axis_index("layer") // (1 << bit) % 2 == 0
    upper = jnp.where(is_upper, state, partner)
    lower = jnp.where(is_upper, partner, state)
    refl_a, trans_a, refl_a_back, trans_a_back = (upper[0], upper[1], upper[2], upper[3])
    refl_b, trans_b, refl_b_back, trans_b_back = (lower[0], lower[1], lower[2], lower[3])
    first_left = jnp.where(is_upper, refl_a_back, refl_b)
    first_right = jnp.where(is_upper, refl_b, refl_a_back)
    chain_base = jnp.where(is_upper, trans_a, trans_b_back)
    across = jnp.where(is_upper, trans_b, trans_a_back)
    final_left = jnp.where(is_upper, trans_a_back, trans_b)
    addend = jnp.where(is_upper, refl_a, refl_b_back)
    full_right, full_base = (
        lax.all_gather(narrow(first_right), "sph", axis=1, tiled=True),
        lax.all_gather(narrow(chain_base), "sph", axis=1, tiled=True),
    )
    first_mix = complex_product(first_left, full_right)
    chain = chain_base + complex_product(first_mix, full_base)
    full_chain = lax.all_gather(narrow(chain), "sph", axis=1, tiled=True)
    bounce = complex_product(first_right, full_chain)
    own_trans = complex_product(across, full_chain)
    full_bounce = lax.all_gather(narrow(bounce), "sph", axis=1, tiled=True)
    own_refl = addend + complex_product(final_left, full_bounce)
    mine = jnp.stack([own_trans, own_refl])
    theirs = partner_2(mine.astype(jnp.bfloat16), "layer", bit).astype(mine.dtype)
    trans_new = jnp.where(is_upper, mine[0], theirs[0])
    refl_new = jnp.where(is_upper, mine[1], theirs[1])
    trans_back_new = jnp.where(is_upper, theirs[0], mine[0])
    refl_back_new = jnp.where(is_upper, theirs[1], mine[1])
    return jnp.stack([refl_new, trans_new, refl_back_new, trans_back_new])


def by_rows(out_basis, in_basis, tmatrix, sites, waves, layer_phase):
    width = 2 * waves.shape[1]
    rows = width // lax.axis_size("sph")
    angles = wave_angles(sites[0], waves)
    factor_set = factors(out_basis[0], in_basis[0], tmatrix[0], angles)
    summed = lax.psum_scatter(
        project_rows(factor_set).astype(jnp.bfloat16), "sph", scatter_dimension=0, tiled=True
    ).astype(jnp.float32)
    first_row = lax.axis_index("sph") * rows
    diagonal = ((first_row + jnp.arange(rows))[:, None] == jnp.arange(width)[None, :]).astype(
        jnp.float32
    )
    refl = jnp.stack([summed[:, :width], summed[:, width : 2 * width]])
    trans_re = summed[:, 2 * width : 3 * width] + diagonal * jnp.cos(layer_phase[0])[None, :]
    trans_im = summed[:, 3 * width :] + diagonal * jnp.sin(layer_phase[0])[None, :]
    trans = jnp.stack([trans_re, trans_im])
    state = jnp.stack([refl, trans, refl, trans])
    levels = lax.axis_size("layer").bit_length() - 1
    for bit in range(levels):
        state = merge_level(state, bit)
    columns = width // lax.axis_size("layer")
    first_column = lax.axis_index("layer") * columns
    own_refl = lax.dynamic_slice_in_dim(state[0], first_column, columns, 2)
    own_trans = lax.dynamic_slice_in_dim(state[1], first_column, columns, 2)
    return (own_refl, own_trans)


def mm(left, right):
    return jnp.dot(left, right, preferred_element_type=F32)


def mm_t(left, right):
    return lax.dot_general(left, right, (((0,), (0,)), ((), ())), preferred_element_type=F32)


def cmul(left, right):
    return (
        mm(left[0], right[0]) - mm(left[1], right[1]),
        mm(left[0], right[1]) + mm(left[1], right[0]),
    )


def half(pair):
    return (pair[0].astype(BF16), pair[1].astype(BF16))


def add(one, two):
    return (one[0] + two[0], one[1] + two[1])


def circle(turns):
    turn = turns * (1.0 / LATTICE)
    turn = turn - jnp.floor(turn)
    quarter = jnp.floor(turn * 4.0 + 0.5)
    x = (turn - quarter * 0.25) * TWO_PI
    y = x * x
    sin = x * (1.0 + y * (-1.0 / 6 + y * (1.0 / 120 + y * (-1.0 / 5040 + y * (1.0 / 362880)))))
    cos = 1.0 + y * (-0.5 + y * (1.0 / 24 + y * (-1.0 / 720 + y * (1.0 / 40320))))
    odd = (quarter == 1.0) | (quarter == 3.0)
    cos, sin = jnp.where(odd, sin, cos), jnp.where(odd, cos, sin)
    cos = jnp.where((quarter == 1.0) | (quarter == 2.0), -cos, cos)
    sin = jnp.where((quarter == 2.0) | (quarter == 3.0), -sin, sin)
    return cos, sin


def layer_kernel(count, spheres, multi, last, *refs):
    sent = refs[:count]
    rest = list(refs[count:])
    out_tile, in_pair, waves = rest[:3]
    rest = rest[3:]
    if last:
        prev_hbm, phase_row = rest[:2]
        rest = rest[2:]
    out = rest[0]
    rest = rest[1:]
    sum_1, sum_2, sum_3, cos_t, sin_t = rest[:5]
    left_slots = (rest[5:8], rest[8:11])
    right_slots = (rest[11:14], rest[14:17])
    spread_slots = (rest[17:19], rest[19:21])
    cos_s, sin_s, blocks_here, block_sem = rest[21:25]
    blocks = [blocks_here.at[index] for index in range(count)]
    copies = [
        pltpu.make_async_copy(sent[index], blocks_here.at[index], block_sem.at[index])
        for index in range(count)
    ]
    for copy in copies:
        copy.start()
    if last:
        prev, arrived = rest[25:]
        fetch = pltpu.make_async_copy(prev_hbm, prev, arrived)
        fetch.start()
    depth = spheres * multi
    half_width = waves.shape[1]
    width = 2 * half_width
    lanes = cos_t.shape[0]
    parts = 1
    tall = 2 * width // parts
    few, size = spheres // parts, depth // parts

    for copy in copies:
        copy.wait()
    coords = None
    for index, block in enumerate(blocks):
        row = lax.broadcasted_iota(jnp.int32, (depth, lanes), 0)
        lane = lax.broadcasted_iota(jnp.int32, (depth, lanes), 1)
        pick = (row == (lane - spheres * index) * multi).astype(F32).astype(BF16)
        part = mm(block[2 * multi : 2 * multi + EXTRA, :], pick)
        coords = part if coords is None else coords + part
    turns = mm_t(waves[...], coords.astype(BF16))
    cos_v, sin_v = circle(turns)
    for index in range(count):
        at = slice(spheres * index, spheres * (index + 1))
        cos_s[index] = cos_v[:, at].astype(BF16)
        sin_s[index] = sin_v[:, at].astype(BF16)
    cos_t[...] = cos_v.T
    sin_t[...] = sin_v.T
    row = lax.broadcasted_iota(jnp.int32, (spheres, depth), 0)
    lane = lax.broadcasted_iota(jnp.int32, (spheres, depth), 1)
    inside = (lane >= row * multi) & (lane < row * multi + multi)
    pick_s = inside.astype(F32).astype(BF16)

    def spread(slot, index, at, many):
        rows = pl.ds(at, many)
        slot[0][rows, :] = mm(cos_s[index, rows, :], pick_s).astype(BF16)
        slot[1][rows, :] = mm(sin_s[index, rows, :], pick_s).astype(BF16)

    def build_left(slot, phases, part, piece):
        low = (piece * tall // 8) % half_width
        many = tall // 8
        c, s = phases[0][low : low + many, :], phases[1][low : low + many, :]
        rows = pl.ds(part * tall + piece * many, many)
        u_re = out_tile[0, rows, :]
        u_im = out_tile[1, rows, :]
        re = u_re * c - u_im * s
        im = u_re * s + u_im * c
        slot[0][rows, :] = re
        slot[1][rows, :] = im
        slot[2][rows, :] = re + im

    def build_right(slot, index, part, piece):
        many = size // 6
        base = part * size + piece * many
        both = mm_t(
            blocks_here[index, 0 : 2 * multi, pl.ds(base, many)], in_pair[...]
        )
        done = 0
        while done < many:
            k = (piece * many + done) // multi
            stop = min((k + 1) * multi - piece * many, many)
            at = spheres * index + part * few + k
            c = cos_t[pl.ds(at, 1), :]
            s = sin_t[pl.ds(at, 1), :]
            to = pl.ds(base + done, stop - done)
            for pol in range(2):
                lo = pol * half_width
                g_re = both[done:stop, lo : lo + half_width]
                g_im = both[done:stop, width + lo : width + lo + half_width]
                re = g_re * c + g_im * s
                im = g_im * c - g_re * s
                slot[0][to, lo : lo + half_width] = re.astype(BF16)
                slot[1][to, lo : lo + half_width] = im.astype(BF16)
                slot[2][to, lo : lo + half_width] = (re + im).astype(BF16)
            done = stop

    def tasks_of(slot_left, phases, slot_right, index, part):
        lefts = [
            functools.partial(build_left, slot_left, phases, part, piece)
            for piece in range(8)
        ]
        rights = [
            functools.partial(build_right, slot_right, index, part, piece)
            for piece in range(6)
        ]
        tasks = []
        while lefts or rights:
            tasks += lefts[:1] + rights[:1]
            lefts, rights = lefts[1:], rights[1:]
        return tasks

    spread(spread_slots[0], 0, 0, half_width)
    if count > 1:
        spread(spread_slots[1], 1, 0, half_width)

    for task in tasks_of(left_slots[0], spread_slots[0], right_slots[0], 0, 0):
        task()
    for total in (sum_1, sum_2, sum_3):
        total[...] = jnp.zeros(total.shape, F32)

    @pl.loop(0, count // 2)
    def _(pair):
        for now in range(2):
            later = 1 - now
            index = 2 * pair + now
            after = jnp.minimum(index + 1, count - 1)
            tasks = tasks_of(left_slots[later], spread_slots[later], right_slots[later], after, 0)
            after = jnp.minimum(index + 2, count - 1)
            tasks.append(functools.partial(spread, spread_slots[now], after, 0, half_width))
            pieces = [
                (total, left, right, slice(lane * 256, (lane + 1) * 256))
                for total, left, right in zip(
                    (sum_1, sum_2, sum_3), left_slots[now], right_slots[now]
                )
                for lane in range(width // 256)
            ]
            for at, (total, left, right, cols) in enumerate(pieces):
                total[:, cols] += mm(left[...], right[:, cols])
                share = -(-len(tasks) // (len(pieces) - at))
                for task in tasks[:share]:
                    task()
                tasks = tasks[share:]

    if last:
        fetch.wait()
    for part in range(4):
        kind, pol = part // 2, part % 2
        rows = pl.ds(part * half_width, half_width)
        re = sum_1[rows, :] - sum_2[rows, :]
        im = sum_3[rows, :] - sum_1[rows, :] - sum_2[rows, :]
        if not last:
            out[0, rows, :] = re
            out[1, rows, :] = im
        else:
            re = re + prev[0, rows, :]
            im = im + prev[1, rows, :]
            if kind == 1:
                at = lax.broadcasted_iota(jnp.int32, (half_width, width), 0) + pol * half_width
                lane = lax.broadcasted_iota(jnp.int32, (half_width, width), 1)
                on = at == lane
                re = re + jnp.where(on, jnp.cos(phase_row[...]), 0.0)
                im = im + jnp.where(on, jnp.sin(phase_row[...]), 0.0)
            to = pl.ds(pol * half_width, half_width)
            out[2 * kind, to, :] = re.astype(BF16)
            out[2 * kind + 1, to, :] = im.astype(BF16)


def pack_kernel(tmatrix, sites, out):
    spheres, _, multi, _ = tmatrix.shape
    depth = spheres * multi
    for c in range(2):
        flat = tmatrix[:, c].reshape(depth, multi)
        out[c * multi : (c + 1) * multi, :] = flat.T.astype(BF16)
    row = lax.broadcasted_iota(jnp.int32, (spheres, depth), 0)
    lane = lax.broadcasted_iota(jnp.int32, (spheres, depth), 1)
    inside = (lane >= row * multi) & (lane < row * multi + multi)
    pick = inside.astype(F32).astype(BF16)
    site = sites[...].astype(F32)
    column = jnp.floor((site + 0.5) * (1.0 / LATTICE))
    along = site - LATTICE * column
    both = jnp.concatenate([column, along, jnp.zeros((EXTRA - 2, spheres), F32)], axis=0)
    out[2 * multi : 2 * multi + EXTRA, :] = mm(both.astype(BF16), pick).astype(BF16)


def pack(tmatrix, sites):
    spheres, _, multi, _ = tmatrix.shape
    return pl.pallas_call(
        pack_kernel,
        out_shape=jax.ShapeDtypeStruct((2 * multi + EXTRA, spheres * multi), BF16),
        in_specs=[VMEM, VMEM],
        out_specs=VMEM,
        name="pack",
    )(tmatrix, sites)


def prepare_kernel(depth, out_basis, in_basis, waves, out_tile, in_pair, waves_pad):
    multi, width = in_basis.shape[1], in_basis.shape[2]
    row = lax.broadcasted_iota(jnp.int32, (multi, depth), 0).astype(F32)
    lane = lax.broadcasted_iota(jnp.int32, (multi, depth), 1).astype(F32)
    lane = lane - multi * jnp.floor((lane + 0.5) * (1.0 / multi))
    pick = (row == lane).astype(F32).astype(BF16)
    for kind in range(2):
        for c in range(2):
            tile = mm_t(out_basis[kind, c].astype(BF16), pick)
            out_tile[c, kind * width : (kind + 1) * width, :] = tile.astype(BF16)
    b_re, b_im = in_basis[0].astype(BF16), in_basis[1].astype(BF16)
    in_pair[0:multi, 0:width] = b_re
    in_pair[0:multi, width : 2 * width] = b_im
    in_pair[multi : 2 * multi, 0:width] = -b_im
    in_pair[multi : 2 * multi, width : 2 * width] = b_re
    pads = jnp.zeros((EXTRA - 2, width // 2), F32)
    waves_pad[...] = jnp.concatenate([waves[...].astype(F32), pads], axis=0).astype(BF16)


def prepare(out_basis, in_basis, waves, spheres):
    multi, width = in_basis.shape[1], in_basis.shape[2]
    depth = spheres * multi
    return pl.pallas_call(
        functools.partial(prepare_kernel, depth),
        out_shape=(
            jax.ShapeDtypeStruct((2, 2 * width, depth), BF16),
            jax.ShapeDtypeStruct((2 * multi, 2 * width), BF16),
            jax.ShapeDtypeStruct((EXTRA, width // 2), BF16),
        ),
        in_specs=[VMEM] * 3,
        out_specs=(VMEM,) * 3,
        compiler_params=pltpu.CompilerParams(vmem_limit_bytes=16 * 2**20),
        cost_estimate=pl.CostEstimate(flops=2**31, bytes_accessed=2**22, transcendentals=0),
        name="prepare",
    )(out_basis, in_basis, waves)


def layer_sum(blocks, spheres, multi, out_tile, in_pair, waves, prev=None, phase=None):
    count = len(blocks)
    last = prev is not None
    depth = spheres * multi
    half_width = waves.shape[1]
    width = 2 * half_width
    lanes = max(128, count * spheres)
    operands = list(blocks) + [out_tile, in_pair, waves]
    specs = [ANY] * count + [VMEM] * 3
    if last:
        operands += [prev, phase.reshape(1, -1)]
        specs += [ANY, VMEM]
        shape = jax.ShapeDtypeStruct((4, width, width), BF16)
    else:
        shape = jax.ShapeDtypeStruct((2, 2 * width, width), F32)
    scratch = [pltpu.VMEM((2 * width, width), F32)] * 3
    scratch += [pltpu.VMEM((lanes, half_width), F32)] * 2
    scratch += [pltpu.VMEM((2 * width, depth), BF16)] * 6
    scratch += [pltpu.VMEM((depth, width), BF16)] * 6
    scratch += [pltpu.VMEM((half_width, depth), BF16)] * 4
    scratch += [pltpu.VMEM((count, half_width, spheres), BF16)] * 2
    scratch += [pltpu.VMEM((count,) + blocks[0].shape, BF16)]
    scratch += [pltpu.SemaphoreType.DMA((count,))]
    if last:
        scratch += [pltpu.VMEM((2, 2 * width, width), F32), pltpu.SemaphoreType.DMA]
    flops = count * 3 * 2 * 2 * width * width * depth
    return pl.pallas_call(
        functools.partial(layer_kernel, count, spheres, multi, last),
        out_shape=shape,
        in_specs=specs,
        out_specs=VMEM,
        scratch_shapes=scratch,
        compiler_params=pltpu.CompilerParams(vmem_limit_bytes=40 * 2**20),
        cost_estimate=pl.CostEstimate(flops=flops, bytes_accessed=2**23, transcendentals=0),
        name="layer_sum",
    )(*operands)


def take_pair(place, own, other, u, v, sems):
    def take(to, source, at):
        return pltpu.make_async_copy(source, to, sems.at[at])

    @pl.when(place[0] == 1)
    def _():
        take(u, own, 0).start()
        take(v, other, 1).start()

    @pl.when(place[0] == 0)
    def _():
        take(u, other, 0).start()
        take(v, own, 1).start()

    take(u, own, 0).wait()
    take(v, own, 1).wait()
    return (u[0], u[1]), (u[2], u[3]), (v[0], v[1]), (v[2], v[3])


def back_kernel(place, own, other, s_out, u, v, sems):
    side = own.shape[1] // 2
    r_u, t_u, r_v, _ = take_pair(place, own, other, u, v, sems)
    mine = pl.ds(pl.multiple_of(place[1] * side, side), side)
    base = (u[2, :, mine], u[3, :, mine])
    up = cmul(r_v, base)
    again = cmul(r_u, half(up))
    again = cmul(r_v, half(again))
    up = half(add(up, again))
    back = cmul(t_u, up)
    for c in range(2):
        s_out[c] = (u[c, :, mine].astype(F32) + back[c]).astype(BF16)


def rows_kernel(rows, place, own, other, after, h_near, h_far, u, v, sems):
    del after
    width = own.shape[1]
    quarter = width // 4
    core = place[1]
    r_u, t_u, r_v, _ = take_pair(place, own, other, u, v, sems)
    near = pl.ds(pl.multiple_of(core * quarter, quarter), quarter)
    far = pl.ds(pl.multiple_of((core + 2) * quarter, quarter), quarter)

    def columns(ref, at):
        return jnp.concatenate([ref[at, :, near], ref[at, :, far]], axis=1)

    base = (columns(v, 2), columns(v, 3))
    chain = cmul(r_u, base)
    chain = cmul(r_v, half(chain))
    chain = half((base[0] + chain[0], base[1] + chain[1]))
    here = cmul(t_u, chain)
    my = pl.ds(pl.multiple_of(place[2] * rows, rows), rows)
    row_t = (v[2, my, :], v[3, my, :])
    w_1 = half(cmul(row_t, r_u))
    k_part = cmul(w_1, chain)
    w_2 = cmul(w_1, r_v)
    w_2 = half((row_t[0] + w_2[0], row_t[1] + w_2[1]))
    g_rows = half(cmul(w_2, t_u))
    for side, (to, cols) in enumerate(((h_near, near), (h_far, far))):
        at = slice(side * quarter, (side + 1) * quarter)
        for c in range(2):
            to[c, 0:width, :] = here[c][:, at].astype(BF16)
            k_side = v[c, my, cols].astype(F32) + k_part[c][:, at]
            to[c, width : width + rows, :] = k_side.astype(BF16)
            for q in range(4):
                put = width + rows + q * rows
                to[c, put : put + rows, :] = g_rows[c][:, q * quarter : (q + 1) * quarter]


def form(place, own, other, rows):
    width = own.shape[1]
    scratch = [pltpu.VMEM(own.shape, BF16)] * 2 + [pltpu.SemaphoreType.DMA((2,))]
    params = pltpu.CompilerParams(vmem_limit_bytes=24 * 2**20)
    back = pl.pallas_call(
        back_kernel,
        out_shape=jax.ShapeDtypeStruct((2, width, width // 2), BF16),
        in_specs=[SMEM, ANY, ANY],
        out_specs=VMEM,
        scratch_shapes=scratch,
        compiler_params=params,
        cost_estimate=pl.CostEstimate(flops=2**32, bytes_accessed=2**23, transcendentals=0),
        name="back",
    )(place, own, other)
    shape = jax.ShapeDtypeStruct((2, width + 5 * rows, width // 4), BF16)
    near, far = pl.pallas_call(
        functools.partial(rows_kernel, rows),
        out_shape=(shape, shape),
        in_specs=[SMEM, ANY, ANY, ANY],
        out_specs=(VMEM, VMEM),
        scratch_shapes=scratch,
        compiler_params=params,
        cost_estimate=pl.CostEstimate(flops=2**32, bytes_accessed=2**23, transcendentals=0),
        name="rows",
    )(place, own, other, back)
    return back, near, far


def join_kernel(
    rows, place, s_mine, s_side, s_far, s_far_side, h_near, h_sent, refl, trans, sides, h, sems
):
    width = sides.shape[3]
    lower, core = place[3], place[1]
    moves = (
        (s_mine, sides.at[lower, core]),
        (s_side, sides.at[lower, 1 - core]),
        (s_far, sides.at[1 - lower, core]),
        (s_far_side, sides.at[1 - lower, 1 - core]),
        (h_near, h.at[lower]),
        (h_sent, h.at[1 - lower]),
    )
    copies = [pltpu.make_async_copy(*move, sems.at[at]) for at, move in enumerate(moves)]
    for copy in copies:
        copy.start()
    for copy in copies:
        copy.wait()

    def rows_of(side):
        return tuple(
            jnp.concatenate(
                [
                    h[side, c, width + rows + q * rows : width + 2 * rows + q * rows, :]
                    for q in range(4)
                ],
                axis=1,
            )
            for c in range(2)
        )

    def times(pair, side):
        parts = [
            cmul(pair, (sides[side, at, 0], sides[side, at, 1]))
            for at in range(2)
        ]
        return tuple(jnp.concatenate([parts[0][c], parts[1][c]], axis=1) for c in range(2))

    from_above = rows_of(0)
    from_below = rows_of(1)
    second = half(times(from_above, 1))
    both = tuple(jnp.concatenate([from_below[c], second[c]], axis=0) for c in range(2))
    chain = times(half(times(both, 0)), 1)
    chain = half(tuple(both[c].astype(F32) + chain[c] for c in range(2)))
    result = cmul(chain, (h[0, 0, 0:width, :], h[0, 1, 0:width, :]))
    for c in range(2):
        trans[c] = result[c][0:rows]
        refl[c] = h[0, c, width : width + rows, :].astype(F32) + result[c][rows : 2 * rows]


def join(place, s_mine, s_side, s_far, s_far_side, h_near, h_sent, rows):
    columns = h_near.shape[2]
    shape = jax.ShapeDtypeStruct((2, rows, columns), F32)
    return pl.pallas_call(
        functools.partial(join_kernel, rows),
        out_shape=(shape, shape),
        in_specs=[SMEM] + [ANY] * 6,
        out_specs=(VMEM, VMEM),
        scratch_shapes=[
            pltpu.VMEM((2, 2) + s_mine.shape, BF16),
            pltpu.VMEM((2,) + h_near.shape, BF16),
            pltpu.SemaphoreType.DMA((6,)),
        ],
        compiler_params=pltpu.CompilerParams(vmem_limit_bytes=20 * 2**20),
        cost_estimate=pl.CostEstimate(flops=2**30, bytes_accessed=2**22, transcendentals=0),
        name="join",
    )(place, s_mine, s_side, s_far, s_far_side, h_near, h_sent)


def whole_layers(inner, out_basis, in_basis, tmatrix, sites, waves, layer_phase):
    spheres, multi = tmatrix.shape[1], tmatrix.shape[3]
    half_width = waves.shape[1]
    width = 2 * half_width
    groups = lax.axis_size("sph")
    outer = groups // inner
    rows = width // groups
    layer = lax.axis_index("layer")

    block = pack(tmatrix[0], sites)

    def shifted(value, far, side):
        pairs = [
            (g, ((g // inner + far) % outer) * inner + (g % inner + side) % inner)
            for g in range(groups)
        ]
        return lax.ppermute(value, "sph", pairs)

    near = [shifted(block, 0, 1), shifted(block, 1, 0), shifted(block, outer - 1, 0)]
    near = [block, *near]
    far = [shifted(block, 2, 0), shifted(near[2], 0, 1), shifted(near[3], 0, 1)]
    far += [shifted(block, 2, 1)]

    ready = prepare(out_basis[0], in_basis[0], waves, spheres)
    part = layer_sum(near, spheres, multi, *ready)
    own = layer_sum(far, spheres, multi, *ready, part, layer_phase[0])

    other = lax.ppermute(own, "layer", [(at, at ^ 1) for at in range(4)])
    core, lower = layer % 2, layer // 2
    mine_is_u = jnp.where(core != lower, 1, 0)
    place = jnp.stack([mine_is_u, core, lax.axis_index("sph"), lower]).astype(jnp.int32)
    s_mine, h_near, h_far = form(place, own, other, rows)
    s_far = lax.ppermute(s_mine, "layer", [(at, at ^ 2) for at in range(4)])
    h_sent = lax.ppermute(h_far, "layer", [(at ^ 2, at) for at in range(4)])
    s_side = lax.ppermute(s_mine, "layer", [(at, at ^ 1) for at in range(4)])
    s_far, h_near = lax.optimization_barrier((s_far, h_near))
    s_far_side = lax.ppermute(s_far, "layer", [(at, at ^ 1) for at in range(4)])
    return join(place, s_mine, s_side, s_far, s_far_side, h_near, h_sent, rows)


def solution(mesh):
    in_specs = (
        P("layer", None, None, None, None),
        P("layer", None, None, None),
        P("layer", "sph", None, None, None),
        P("layer", "sph"),
        P(),
        P("layer", None),
    )
    out_specs = (P(None, "sph", "layer"), P(None, "sph", "layer"))
    on_device = by_rows
    if mesh.shape["layer"] == 4 and mesh.shape["sph"] == 8:
        on_device = functools.partial(whole_layers, 2)
    return jax.shard_map(
        on_device, mesh=mesh, in_specs=in_specs, out_specs=out_specs, check_vma=False
    )
```

profile of v0, /device:TPU:8, one launch (start us, length us, event | category | flops | bytes accessed | tf_op | source)
XLA Modules:
  0.0 106.1 jit_solution(4821113638780015240)
XLA Ops:
  0.6 2.0 %pack.1.refs_0_ = bf16[112,768]{1,0:T(8,128)(2,1)} custom-call(f32[16,2,48,48]{3,2,1,0:T(8,128)} %bitcast.9, s32[1,16]{1,0:T(1,128)} %sites.1), custom_call_target="tpu_custom_call" | custom-call | tf_op jit(solution)/shard_map/pack/pallas_call | solution.py:383
  2.6 1.5 %collective-permute-start.6 = (bf16[112,768]{1,0:T(8,128)(2,1)}, bf16[112,768]{1,0:T(8,128)(2,1)S(1)}, u32[]{:S(2)}, u32[]{:S(2)}) collective-permute-start(bf16[112,768]{1,0:T(8,128)(2,1)} %pack.1.refs_0_), channel_id=1, source_target_pairs={{0,1},{1,0},{2,3},{3,2},{4,5},{5,4},{6,7},{7,6},{8,9},{9,8},{10,11... | collective-permute-start | bytes 516104 | tf_op jit(solution)/shard_map/ppermute | solution.py:648
  4.1 2.5 %collective-permute-start.5 = (bf16[112,768]{1,0:T(8,128)(2,1)}, bf16[112,768]{1,0:T(8,128)(2,1)S(1)}, u32[]{:S(2)}, u32[]{:S(2)}) collective-permute-start(bf16[112,768]{1,0:T(8,128)(2,1)} %pack.1.refs_0_), channel_id=1, source_target_pairs={{0,5},{1,4},{2,7},{3,6},{4,1},{5,0},{6,3},{7,2},{8,13},{9,12},{10,... | collective-permute-start | bytes 516104 | tf_op jit(solution)/shard_map/ppermute | solution.py:648
  6.6 0.4 collective-permute-start.3
  7.1 1.6 %collective-permute-start.1 = (bf16[112,768]{1,0:T(8,128)(2,1)}, bf16[112,768]{1,0:T(8,128)(2,1)S(1)}, u32[]{:S(2)}, u32[]{:S(2)}) collective-permute-start(bf16[112,768]{1,0:T(8,128)(2,1)} %pack.1.refs_0_), channel_id=1, source_target_pairs={{0,2},{1,3},{2,4},{3,5},{4,6},{5,7},{6,0},{7,1},{8,10},{9,11},{10,... | collective-permute-start | bytes 516104 | tf_op jit(solution)/shard_map/ppermute | solution.py:648
  8.7 2.1 %collective-permute-start = (bf16[112,768]{1,0:T(8,128)(2,1)}, bf16[112,768]{1,0:T(8,128)(2,1)S(1)}, u32[]{:S(2)}, u32[]{:S(2)}) collective-permute-start(bf16[112,768]{1,0:T(8,128)(2,1)} %pack.1.refs_0_), channel_id=1, source_target_pairs={{0,4},{1,5},{2,6},{3,7},{4,0},{5,1},{6,2},{7,3},{8,12},{9,13},{10,... | collective-permute-start | bytes 516104 | tf_op jit(solution)/shard_map/ppermute | solution.py:648
  10.8 1.0 copy-done.1
  11.8 0.9 copy-done.2
  12.7 0.7 copy-done.3
  13.4 1.0 prepare.1
  14.4 11.5 %collective-permute-done.3.refs_3_ = bf16[112,768]{1,0:T(8,128)(2,1)S(1)} collective-permute-done((bf16[112,768]{1,0:T(8,128)(2,1)}, bf16[112,768]{1,0:T(8,128)(2,1)S(1)}, u32[]{:S(2)}, u32[]{:S(2)}) %collective-permute-start.3) | collective-permute-done | bytes 172064 | tf_op jit(solution)/shard_map/ppermute | solution.py:648
  25.9 1.5 %collective-permute-start.4 = (bf16[112,768]{1,0:T(8,128)(2,1)S(1)}, bf16[112,768]{1,0:T(8,128)(2,1)S(1)}, u32[]{:S(2)}, u32[]{:S(2)}) collective-permute-start(bf16[112,768]{1,0:T(8,128)(2,1)S(1)} %collective-permute-done.3.refs_3_), channel_id=1, source_target_pairs={{0,1},{1,0},{2,3},{3,2},{4,5},{5,4},{6,7},{7,6},{8,9},{9,8},{10,11... | collective-permute-start | bytes 516104 | tf_op jit(solution)/shard_map/ppermute | solution.py:648
  27.4 0.5 collective-permute-start.2
  27.9 0.0 collective-permute-done.6.refs_1_
  27.9 19.2 %layer_sum.2.refs_7_ = f32[2,1024,512]{2,1,0:T(8,128)S(1)} custom-call(bf16[112,768]{1,0:T(8,128)(2,1)S(1)} %copy-done, bf16[112,768]{1,0:T(8,128)(2,1)S(1)} %collective-permute-done.6.refs_1_, bf16[112,768]{1,0:T(8,128)(2,1)S(1)} %collective-permute-done.1.refs_2_, bf16[112,768]{1,0:T(8,128)(2,1)S(1)} %collective-permute-done.3.refs_3_, ...), custom_call_target="tpu_custom_call" | custom-call | flops 9663676416 | bytes 8388608 | tf_op jit(solution)/shard_map/layer_sum/pallas_call | solution.py:455
  47.1 0.0 collective-permute-done.5.refs_3_
  47.1 0.0 collective-permute-done.2.refs_1_
  47.2 19.9 %layer_sum.3.own = bf16[4,512,512]{2,1,0:T(8,128)(2,1)S(1)} custom-call(bf16[112,768]{1,0:T(8,128)(2,1)S(1)} %collective-permute-done.refs_0_, bf16[112,768]{1,0:T(8,128)(2,1)S(1)} %collective-permute-done.2.refs_1_, bf16[112,768]{1,0:T(8,128)(2,1)S(1)} %collective-permute-done.4.refs_2_, bf16[112,768]{1,0:T(8,128)(2,1)S(1)} %collective-permute-done.5.refs_3_, ...), custom_call_target="tpu_custom_call" | custom-call | flops 9663676416 | bytes 8388608 | tf_op jit(solution)/shard_map/layer_sum/pallas_call | solution.py:455
  67.1 0.1 collective-permute-start.7
  67.2 0.1 pad_add_fusion.place
  67.3 4.2 %collective-permute-done.7.other = bf16[4,512,512]{2,1,0:T(8,128)(2,1)} collective-permute-done((bf16[4,512,512]{2,1,0:T(8,128)(2,1)S(1)}, bf16[4,512,512]{2,1,0:T(8,128)(2,1)}, u32[]{:S(2)}, u32[]{:S(2)}) %collective-permute-start.7) | collective-permute-done | bytes 2097184 | tf_op jit(solution)/shard_map/ppermute | solution.py:659
  71.4 4.7 %back.1.after.s_mine = bf16[2,512,256]{2,1,0:T(8,128)(2,1)S(1)} custom-call(s32[4]{0:T(128)S(1)} %pad_add_fusion.place, bf16[4,512,512]{2,1,0:T(8,128)(2,1)S(1)} %layer_sum.3.own, bf16[4,512,512]{2,1,0:T(8,128)(2,1)} %collective-permute-done.7.other), custom_call_target="tpu_custom_call" | custom-call | flops 4294967296 | bytes 8388608 | tf_op jit(solution)/shard_map/back/pallas_call | solution.py:539
  76.2 1.7 %collective-permute-start.9 = (bf16[2,512,256]{2,1,0:T(8,128)(2,1)S(1)}, bf16[2,512,256]{2,1,0:T(8,128)(2,1)S(1)}, u32[]{:S(2)}, u32[]{:S(2)}) collective-permute-start(bf16[2,512,256]{2,1,0:T(8,128)(2,1)S(1)} %back.1.after.s_mine), channel_id=1, source_target_pairs={{0,16},{8,24},{16,0},{24,8},{1,17},{9,25},{17,1},{25,9},{2,18},{10... | collective-permute-start | bytes 1572872 | tf_op jit(solution)/shard_map/ppermute | solution.py:664
  77.9 0.0 collective-permute-start.8
  77.9 5.5 %rows.1 = (bf16[2,832,128]{2,1,0:T(8,128)(2,1)S(1)}, bf16[2,832,128]{2,1,0:T(8,128)(2,1)S(1)}) custom-call(s32[4]{0:T(128)S(1)} %pad_add_fusion.place, bf16[4,512,512]{2,1,0:T(8,128)(2,1)S(1)} %layer_sum.3.own, bf16[4,512,512]{2,1,0:T(8,128)(2,1)} %collective-permute-done.7.other, bf16[2,512,256]{2,1,0:T(8,128)(2,1)S(1)} %back.1.after.s_mine), custom_call_target="tpu_custom_call" | custom-call | flops 4294967296 | bytes 8388608 | tf_op jit(solution)/shard_map/rows/pallas_call | solution.py:550
  83.4 6.9 %collective-permute-done.9.s_far = bf16[2,512,256]{2,1,0:T(8,128)(2,1)S(1)} collective-permute-done((bf16[2,512,256]{2,1,0:T(8,128)(2,1)S(1)}, bf16[2,512,256]{2,1,0:T(8,128)(2,1)S(1)}, u32[]{:S(2)}, u32[]{:S(2)}) %collective-permute-start.9) | collective-permute-done | bytes 524320 | tf_op jit(solution)/shard_map/ppermute | solution.py:664
  90.4 0.0 collective-permute-start.10
  90.4 1.4 %collective-permute-start.11 = (bf16[2,832,128]{2,1,0:T(8,128)(2,1)S(1)}, bf16[2,832,128]{2,1,0:T(8,128)(2,1)S(1)}, u32[]{:S(2)}, u32[]{:S(2)}) collective-permute-start(bf16[2,832,128]{2,1,0:T(8,128)(2,1)S(1)} %get-tuple-element.15), channel_id=1, source_target_pairs={{16,0},{24,8},{0,16},{8,24},{17,1},{25,9},{1,17},{9,25},{18,2},{26... | collective-permute-start | bytes 1277960 | tf_op jit(solution)/shard_map/ppermute | solution.py:665
  91.7 10.9 %collective-permute-done.11.h_sent = bf16[2,832,128]{2,1,0:T(8,128)(2,1)S(1)} collective-permute-done((bf16[2,832,128]{2,1,0:T(8,128)(2,1)S(1)}, bf16[2,832,128]{2,1,0:T(8,128)(2,1)S(1)}, u32[]{:S(2)}, u32[]{:S(2)}) %collective-permute-start.11) | collective-permute-done | bytes 426016 | tf_op jit(solution)/shard_map/ppermute | solution.py:665
  102.6 0.0 collective-permute-done.8.s_side
  102.6 0.0 collective-permute-done.10.s_far_side
  102.6 3.3 %join.1 = (f32[2,64,128]{2,1,0:T(8,128)}, f32[2,64,128]{2,1,0:T(8,128)}) custom-call(s32[4]{0:T(128)S(1)} %pad_add_fusion.place, bf16[2,512,256]{2,1,0:T(8,128)(2,1)S(1)} %back.1.after.s_mine, bf16[2,512,256]{2,1,0:T(8,128)(2,1)S(1)} %collective-permute-done.8.s_side, bf16[2,512,256]{2,1,0:T(8,128)(2,1)S(1)} %collective-permute-done.9.s_far, ...), custom_call_target="tpu_custom_call" | custom-call | flops 1073741824 | bytes 4194304 | tf_op jit(solution)/shard_map/join/pallas_call | solution.py:616
  (10 shorter events, 0.0 us)
Async XLA Ops:
  2.6 25.3 %collective-permute-start.6 = (bf16[112,768]{1,0:T(8,128)(2,1)}, bf16[112,768]{1,0:T(8,128)(2,1)S(1)}, u32[]{:S(2)}, u32[]{:S(2)}) collective-permute-start(bf16[112,768]{1,0:T(8,128)(2,1)} %pack.1.refs_0_), channel_id=1, source_target_pairs={{0,1},{1,0},{2,3},{3,2},{4,5},{5,4},{6,7},{7,6},{8,9},{9,8},{10,11... | collective-permute-start | bytes 516104 | tf_op jit(solution)/shard_map/ppermute | solution.py:648
  4.1 43.0 %collective-permute-start.5 = (bf16[112,768]{1,0:T(8,128)(2,1)}, bf16[112,768]{1,0:T(8,128)(2,1)S(1)}, u32[]{:S(2)}, u32[]{:S(2)}) collective-permute-start(bf16[112,768]{1,0:T(8,128)(2,1)} %pack.1.refs_0_), channel_id=1, source_target_pairs={{0,5},{1,4},{2,7},{3,6},{4,1},{5,0},{6,3},{7,2},{8,13},{9,12},{10,... | collective-permute-start | bytes 516104 | tf_op jit(solution)/shard_map/ppermute | solution.py:648
  6.6 19.2 %collective-permute-start.3 = (bf16[112,768]{1,0:T(8,128)(2,1)}, bf16[112,768]{1,0:T(8,128)(2,1)S(1)}, u32[]{:S(2)}, u32[]{:S(2)}) collective-permute-start(bf16[112,768]{1,0:T(8,128)(2,1)} %pack.1.refs_0_), channel_id=1, source_target_pairs={{0,6},{1,7},{2,0},{3,1},{4,2},{5,3},{6,4},{7,5},{8,14},{9,15},{10,... | collective-permute-start | bytes 516104 | tf_op jit(solution)/shard_map/ppermute | solution.py:648
  7.1 20.3 %collective-permute-start.1 = (bf16[112,768]{1,0:T(8,128)(2,1)}, bf16[112,768]{1,0:T(8,128)(2,1)S(1)}, u32[]{:S(2)}, u32[]{:S(2)}) collective-permute-start(bf16[112,768]{1,0:T(8,128)(2,1)} %pack.1.refs_0_), channel_id=1, source_target_pairs={{0,2},{1,3},{2,4},{3,5},{4,6},{5,7},{6,0},{7,1},{8,10},{9,11},{10,... | collective-permute-start | bytes 516104 | tf_op jit(solution)/shard_map/ppermute | solution.py:648
  8.7 38.5 %collective-permute-start = (bf16[112,768]{1,0:T(8,128)(2,1)}, bf16[112,768]{1,0:T(8,128)(2,1)S(1)}, u32[]{:S(2)}, u32[]{:S(2)}) collective-permute-start(bf16[112,768]{1,0:T(8,128)(2,1)} %pack.1.refs_0_), channel_id=1, source_target_pairs={{0,4},{1,5},{2,6},{3,7},{4,0},{5,1},{6,2},{7,3},{8,12},{9,13},{10,... | collective-permute-start | bytes 516104 | tf_op jit(solution)/shard_map/ppermute | solution.py:648
  10.8 1.0 copy-start.1
  11.8 0.9 copy-start.2
  12.7 0.7 copy-start.3
  13.4 14.5 %copy-start = (bf16[112,768]{1,0:T(8,128)(2,1)S(1)}, bf16[112,768]{1,0:T(8,128)(2,1)}, u32[]{:S(2)}) copy-start(bf16[112,768]{1,0:T(8,128)(2,1)} %pack.1.refs_0_) | copy-start | bytes 516100
  25.9 21.2 %collective-permute-start.4 = (bf16[112,768]{1,0:T(8,128)(2,1)S(1)}, bf16[112,768]{1,0:T(8,128)(2,1)S(1)}, u32[]{:S(2)}, u32[]{:S(2)}) collective-permute-start(bf16[112,768]{1,0:T(8,128)(2,1)S(1)} %collective-permute-done.3.refs_3_), channel_id=1, source_target_pairs={{0,1},{1,0},{2,3},{3,2},{4,5},{5,4},{6,7},{7,6},{8,9},{9,8},{10,11... | collective-permute-start | bytes 516104 | tf_op jit(solution)/shard_map/ppermute | solution.py:648
  27.4 19.7 %collective-permute-start.2 = (bf16[112,768]{1,0:T(8,128)(2,1)S(1)}, bf16[112,768]{1,0:T(8,128)(2,1)S(1)}, u32[]{:S(2)}, u32[]{:S(2)}) collective-permute-start(bf16[112,768]{1,0:T(8,128)(2,1)S(1)} %collective-permute-done.1.refs_2_), channel_id=1, source_target_pairs={{0,1},{1,0},{2,3},{3,2},{4,5},{5,4},{6,7},{7,6},{8,9},{9,8},{10,11... | collective-permute-start | bytes 516104 | tf_op jit(solution)/shard_map/ppermute | solution.py:648
  27.9 19.2 %copy-start.4 = (f32[1,512]{1,0:T(1,128)S(1)}, f32[1,512]{1,0:T(1,128)}, u32[]{:S(2)}) copy-start(f32[1,512]{1,0:T(1,128)} %refs_8_.1) | copy-start | bytes 6148
  67.1 4.4 %collective-permute-start.7 = (bf16[4,512,512]{2,1,0:T(8,128)(2,1)S(1)}, bf16[4,512,512]{2,1,0:T(8,128)(2,1)}, u32[]{:S(2)}, u32[]{:S(2)}) collective-permute-start(bf16[4,512,512]{2,1,0:T(8,128)(2,1)S(1)} %layer_sum.3.own), channel_id=1, source_target_pairs={{0,8},{8,0},{16,24},{24,16},{1,9},{9,1},{17,25},{25,17},{2,10},{10... | collective-permute-start | bytes 6291464 | tf_op jit(solution)/shard_map/ppermute | solution.py:659
  76.2 14.2 %collective-permute-start.9 = (bf16[2,512,256]{2,1,0:T(8,128)(2,1)S(1)}, bf16[2,512,256]{2,1,0:T(8,128)(2,1)S(1)}, u32[]{:S(2)}, u32[]{:S(2)}) collective-permute-start(bf16[2,512,256]{2,1,0:T(8,128)(2,1)S(1)} %back.1.after.s_mine), channel_id=1, source_target_pairs={{0,16},{8,24},{16,0},{24,8},{1,17},{9,25},{17,1},{25,9},{2,18},{10... | collective-permute-start | bytes 1572872 | tf_op jit(solution)/shard_map/ppermute | solution.py:664
  77.9 24.7 %collective-permute-start.8 = (bf16[2,512,256]{2,1,0:T(8,128)(2,1)S(1)}, bf16[2,512,256]{2,1,0:T(8,128)(2,1)S(1)}, u32[]{:S(2)}, u32[]{:S(2)}) collective-permute-start(bf16[2,512,256]{2,1,0:T(8,128)(2,1)S(1)} %back.1.after.s_mine), channel_id=1, source_target_pairs={{0,8},{8,0},{16,24},{24,16},{1,9},{9,1},{17,25},{25,17},{2,10},{10... | collective-permute-start | bytes 1572872 | tf_op jit(solution)/shard_map/ppermute | solution.py:666
  90.4 12.2 %collective-permute-start.10 = (bf16[2,512,256]{2,1,0:T(8,128)(2,1)S(1)}, bf16[2,512,256]{2,1,0:T(8,128)(2,1)S(1)}, u32[]{:S(2)}, u32[]{:S(2)}) collective-permute-start(bf16[2,512,256]{2,1,0:T(8,128)(2,1)S(1)} %collective-permute-done.9.s_far), channel_id=1, source_target_pairs={{0,8},{8,0},{16,24},{24,16},{1,9},{9,1},{17,25},{25,17},{2,10},{10... | collective-permute-start | bytes 1572872 | tf_op jit(solution)/shard_map/ppermute | solution.py:668
  90.4 12.2 %collective-permute-start.11 = (bf16[2,832,128]{2,1,0:T(8,128)(2,1)S(1)}, bf16[2,832,128]{2,1,0:T(8,128)(2,1)S(1)}, u32[]{:S(2)}, u32[]{:S(2)}) collective-permute-start(bf16[2,832,128]{2,1,0:T(8,128)(2,1)S(1)} %get-tuple-element.15), channel_id=1, source_target_pairs={{16,0},{24,8},{0,16},{8,24},{17,1},{25,9},{1,17},{9,25},{18,2},{26... | collective-permute-start | bytes 1277960 | tf_op jit(solution)/shard_map/ppermute | solution.py:665
where the time goes:
time: 106 us
  Pallas kernels  55.6 us (52%)
  waiting for transfers between devices  33.5 us (32%)
  starting transfers between devices  13.4 us (13%)
  local copies, waits for them, and re-layouts  2.61 us (2%)
    pallas_call x2, Pallas kernels, layer_sum(): pl.pallas_call(functools.partial(layer_kernel, count, spheres, multi, las...  39.1 us
    ppermute x7, waiting for transfers between devices, shifted(): return lax.ppermute(value, 'sph', pairs)  11.5 us
    ppermute x1, waiting for transfers between devices, whole_layers(): h_sent = lax.ppermute(h_far, 'layer', [(at ^ 2, at) for at in range(4)])  10.9 us
    ppermute x7, starting transfers between devices, shifted(): return lax.ppermute(value, 'sph', pairs)  10.2 us
    ppermute x1, waiting for transfers between devices, whole_layers(): s_far = lax.ppermute(s_mine, 'layer', [(at, at ^ 2) for at in range(4)])  6.93 us
    pallas_call x1, Pallas kernels, form(): pl.pallas_call(functools.partial(rows_kernel, rows), out_shape=(shape, sh...  5.52 us
    pallas_call x1, Pallas kernels, form(): pl.pallas_call(back_kernel, out_shape=jax.ShapeDtypeStruct((2, width, wid...  4.74 us
    ppermute x1, waiting for transfers between devices, whole_layers(): other = lax.ppermute(own, 'layer', [(at, at ^ 1) for at in range(4)])  4.18 us
  transfers between devices with their start and end apart: 12, of which 4 were waited for; matrix products, arithmetic and copies ran while one was open for 0% of the time, Pallas kernels for 24%

commit v1 on v0

--- a/solution.py
+++ b/solution.py
@@ -311,9 +311,6 @@
 
     for task in tasks_of(left_slots[0], spread_slots[0], right_slots[0], 0, 0):
         task()
-    for total in (sum_1, sum_2, sum_3):
-        total[...] = jnp.zeros(total.shape, F32)
-
     @pl.loop(0, count // 2)
     def _(pair):
         for now in range(2):
@@ -331,7 +328,10 @@
                 for lane in range(width // 256)
             ]
             for at, (total, left, right, cols) in enumerate(pieces):
-                total[:, cols] += mm(left[...], right[:, cols])
+                before = total[:, cols]
+                if now == 0:
+                    before = jnp.where(pair > 0, before, 0.0)
+                total[:, cols] = before + mm(left[...], right[:, cols])
                 share = -(-len(tasks) // (len(pieces) - at))
                 for task in tasks[:share]:
                     task()
@@ -483,7 +483,7 @@
     return (u[0], u[1]), (u[2], u[3]), (v[0], v[1]), (v[2], v[3])
 
 
-def back_kernel(place, own, other, s_out, u, v, sems):
+def back_kernel(place, own, other, s_out, s_send, u, v, sems):
     side = own.shape[1] // 2
     r_u, t_u, r_v, _ = take_pair(place, own, other, u, v, sems)
     mine = pl.ds(pl.multiple_of(place[1] * side, side), side)
@@ -495,6 +495,7 @@
     back = cmul(t_u, up)
     for c in range(2):
         s_out[c] = (u[c, :, mine].astype(F32) + back[c]).astype(BF16)
+        s_send[c] = s_out[c, pl.ds(pl.multiple_of(place[4] * side, side), side), :]
 
 
 def rows_kernel(rows, place, own, other, after, h_near, h_far, u, v, sems):
@@ -536,11 +537,14 @@
     width = own.shape[1]
     scratch = [pltpu.VMEM(own.shape, BF16)] * 2 + [pltpu.SemaphoreType.DMA((2,))]
     params = pltpu.CompilerParams(vmem_limit_bytes=24 * 2**20)
-    back = pl.pallas_call(
+    back, send = pl.pallas_call(
         back_kernel,
-        out_shape=jax.ShapeDtypeStruct((2, width, width // 2), BF16),
+        out_shape=(
+            jax.ShapeDtypeStruct((2, width, width // 2), BF16),
+            jax.ShapeDtypeStruct((2, width // 2, width // 2), BF16),
+        ),
         in_specs=[SMEM, ANY, ANY],
-        out_specs=VMEM,
+        out_specs=(VMEM, VMEM),
         scratch_shapes=scratch,
         compiler_params=params,
         cost_estimate=pl.CostEstimate(flops=2**32, bytes_accessed=2**23, transcendentals=0),
@@ -557,19 +561,24 @@
         cost_estimate=pl.CostEstimate(flops=2**32, bytes_accessed=2**23, transcendentals=0),
         name="rows",
     )(place, own, other, back)
-    return back, near, far
+    return back, send, near, far
 
 
 def join_kernel(
-    rows, place, s_mine, s_side, s_far, s_far_side, h_near, h_sent, refl, trans, sides, h, sems
+    rows, place, s_mine, s_side, q_0, q_1, q_2, q_3, h_near, h_sent, refl, trans, sides, h, sems
 ):
     width = sides.shape[3]
     lower, core = place[3], place[1]
+    many = width // 2
+    this = pl.ds(pl.multiple_of(place[4] * many, many), many)
+    that = pl.ds(pl.multiple_of((1 - place[4]) * many, many), many)
     moves = (
         (s_mine, sides.at[lower, core]),
         (s_side, sides.at[lower, 1 - core]),
-        (s_far, sides.at[1 - lower, core]),
-        (s_far_side, sides.at[1 - lower, 1 - core]),
+        (q_0, sides.at[1 - lower, core, :, this, :]),
+        (q_1, sides.at[1 - lower, core, :, that, :]),
+        (q_2, sides.at[1 - lower, 1 - core, :, this, :]),
+        (q_3, sides.at[1 - lower, 1 - core, :, that, :]),
         (h_near, h.at[lower]),
         (h_sent, h.at[1 - lower]),
     )
@@ -610,23 +619,23 @@
         refl[c] = h[0, c, width : width + rows, :].astype(F32) + result[c][rows : 2 * rows]
 
 
-def join(place, s_mine, s_side, s_far, s_far_side, h_near, h_sent, rows):
+def join(place, s_mine, s_side, quarters, h_near, h_sent, rows):
     columns = h_near.shape[2]
     shape = jax.ShapeDtypeStruct((2, rows, columns), F32)
     return pl.pallas_call(
         functools.partial(join_kernel, rows),
         out_shape=(shape, shape),
-        in_specs=[SMEM] + [ANY] * 6,
+        in_specs=[SMEM] + [ANY] * 8,
         out_specs=(VMEM, VMEM),
         scratch_shapes=[
             pltpu.VMEM((2, 2) + s_mine.shape, BF16),
             pltpu.VMEM((2,) + h_near.shape, BF16),
-            pltpu.SemaphoreType.DMA((6,)),
+            pltpu.SemaphoreType.DMA((8,)),
         ],
         compiler_params=pltpu.CompilerParams(vmem_limit_bytes=20 * 2**20),
         cost_estimate=pl.CostEstimate(flops=2**30, bytes_accessed=2**22, transcendentals=0),
         name="join",
-    )(place, s_mine, s_side, s_far, s_far_side, h_near, h_sent)
+    )(place, s_mine, s_side, *quarters, h_near, h_sent)
 
 
 def whole_layers(inner, out_basis, in_basis, tmatrix, sites, waves, layer_phase):
@@ -649,24 +658,33 @@
 
     near = [shifted(block, 0, 1), shifted(block, 1, 0), shifted(block, outer - 1, 0)]
     near = [block, *near]
-    far = [shifted(block, 2, 0), shifted(near[2], 0, 1), shifted(near[3], 0, 1)]
-    far += [shifted(block, 2, 1)]
-
-    ready = prepare(out_basis[0], in_basis[0], waves, spheres)
+    tile, pair, waves_pad = prepare(out_basis[0], in_basis[0], waves, spheres)
+    late, waves_pad = lax.optimization_barrier((block, waves_pad))
+    ready = (tile, pair, waves_pad)
+    far = [shifted(late, 2, 0), shifted(near[2], 0, 1), shifted(near[3], 0, 1)]
+    far += [shifted(late, 2, 1)]
+
     part = layer_sum(near, spheres, multi, *ready)
     own = layer_sum(far, spheres, multi, *ready, part, layer_phase[0])
 
     other = lax.ppermute(own, "layer", [(at, at ^ 1) for at in range(4)])
     core, lower = layer % 2, layer // 2
     mine_is_u = jnp.where(core != lower, 1, 0)
-    place = jnp.stack([mine_is_u, core, lax.axis_index("sph"), lower]).astype(jnp.int32)
-    s_mine, h_near, h_far = form(place, own, other, rows)
-    s_far = lax.ppermute(s_mine, "layer", [(at, at ^ 2) for at in range(4)])
-    h_sent = lax.ppermute(h_far, "layer", [(at ^ 2, at) for at in range(4)])
-    s_side = lax.ppermute(s_mine, "layer", [(at, at ^ 1) for at in range(4)])
+    group = lax.axis_index("sph")
+    side = group % inner
+    place = jnp.stack([mine_is_u, core, group, lower, side]).astype(jnp.int32)
+    s_mine, s_send, h_near, h_far = form(place, own, other, rows)
+
+    def crossed(value, bit):
+        return lax.ppermute(value, "layer", [(at, at ^ bit) for at in range(4)])
+
+    s_far = crossed(s_send, 2)
+    h_sent = crossed(h_far, 2)
+    s_side = crossed(s_mine, 1)
     s_far, h_near = lax.optimization_barrier((s_far, h_near))
-    s_far_side = lax.ppermute(s_far, "layer", [(at, at ^ 1) for at in range(4)])
-    return join(place, s_mine, s_side, s_far, s_far_side, h_near, h_sent, rows)
+    s_next = shifted(s_far, 0, 1)
+    quarters = (s_far, s_next, crossed(s_far, 1), crossed(s_next, 1))
+    return join(place, s_mine, s_side, quarters, h_near, h_sent, rows)
 
 
 def solution(mesh):

time: 106 us -> 91.3 us (0.86)
  the two profiles are of different devices: /device:TPU:8 before, /device:TPU:0 now
where the time goes in v1:
time: 91.3 us; the launch traced here: 91.1 us
  Pallas kernels  55.3 us (61%)
  starting transfers between devices  16.2 us (18%)
  waiting for transfers between devices  16 us (18%)
  local copies, waits for them, and re-layouts  2.7 us (3%)
  between operations  0.95 us (1%)
    pallas_call x2, Pallas kernels, layer_sum(): pl.pallas_call(functools.partial(layer_kernel, count, spheres, multi, las...  38.7 us
    ppermute x8, starting transfers between devices, shifted(): return lax.ppermute(value, 'sph', pairs)  13 us
    ppermute x5, waiting for transfers between devices, crossed(): return lax.ppermute(value, 'layer', [(at, at ^ bit) for at in range(4)])  6.09 us
    ppermute x8, waiting for transfers between devices, shifted(): return lax.ppermute(value, 'sph', pairs)  5.7 us
    pallas_call x1, Pallas kernels, form(): pl.pallas_call(functools.partial(rows_kernel, rows), out_shape=(shape, sh...  5.52 us
    pallas_call x1, Pallas kernels, form(): pl.pallas_call(back_kernel, out_shape=(jax.ShapeDtypeStruct((2, width, wi...  4.78 us
    ppermute x1, waiting for transfers between devices, whole_layers(): other = lax.ppermute(own, 'layer', [(at, at ^ 1) for at in range(4)])  4.16 us
    pallas_call x1, Pallas kernels, join(): pl.pallas_call(functools.partial(join_kernel, rows), out_shape=(shape, sh...  3.32 us
  transfers between devices with their start and end apart: 14, of which 5 were waited for; matrix products, arithmetic and copies ran while one was open for 0% of the time, Pallas kernels for 28%

profile of v1, /device:TPU:0, one launch (start us, length us, event | category | flops | bytes accessed | tf_op | source)
XLA Modules:
  0.0 91.1 jit_solution(17806444315385731441)
XLA Ops:
  0.6 1.9 %pack.1.refs_0_ = bf16[112,768]{1,0:T(8,128)(2,1)} custom-call(f32[16,2,48,48]{3,2,1,0:T(8,128)} %bitcast.10, s32[1,16]{1,0:T(1,128)} %sites.1), custom_call_target="tpu_custom_call" | custom-call | tf_op jit(solution)/shard_map/pack/pallas_call | solution.py:383
  2.6 3.0 %collective-permute-start.6 = (bf16[112,768]{1,0:T(8,128)(2,1)}, bf16[112,768]{1,0:T(8,128)(2,1)S(1)}, u32[]{:S(2)}, u32[]{:S(2)}) collective-permute-start(bf16[112,768]{1,0:T(8,128)(2,1)} %pack.1.refs_0_), channel_id=1, source_target_pairs={{0,1},{1,0},{2,3},{3,2},{4,5},{5,4},{6,7},{7,6},{8,9},{9,8},{10,11... | collective-permute-start | bytes 516104 | tf_op jit(solution)/shard_map/ppermute | solution.py:657
  5.5 3.6 %collective-permute-start.3 = (bf16[112,768]{1,0:T(8,128)(2,1)}, bf16[112,768]{1,0:T(8,128)(2,1)S(1)}, u32[]{:S(2)}, u32[]{:S(2)}) collective-permute-start(bf16[112,768]{1,0:T(8,128)(2,1)} %pack.1.refs_0_), channel_id=1, source_target_pairs={{0,6},{1,7},{2,0},{3,1},{4,2},{5,3},{6,4},{7,5},{8,14},{9,15},{10,... | collective-permute-start | bytes 516104 | tf_op jit(solution)/shard_map/ppermute | solution.py:657
  9.2 1.0 %copy-done.1 = f32[1,2,2,48,512]{4,3,2,1,0:T(8,128)S(1)} copy-done((f32[1,2,2,48,512]{4,3,2,1,0:T(8,128)S(1)}, f32[1,2,2,48,512]{4,3,2,1,0:T(8,128)}, u32[]{:S(2)}) %copy-start.1) | copy-done | bytes 393240
  10.2 0.9 %copy-done.2 = f32[1,2,48,512]{3,2,1,0:T(8,128)S(1)} copy-done((f32[1,2,48,512]{3,2,1,0:T(8,128)S(1)}, f32[1,2,48,512]{3,2,1,0:T(8,128)}, u32[]{:S(2)}) %copy-start.2) | copy-done | bytes 196632
  11.1 0.7 copy-done.3
  11.8 1.0 %prepare.1 = (bf16[2,1024,768]{2,1,0:T(8,128)(2,1)S(1)}, bf16[96,1024]{1,0:T(8,128)(2,1)S(1)}, bf16[16,256]{1,0:T(8,128)(2,1)S(1)}) custom-call(f32[2,2,48,512]{3,2,1,0:T(8,128)S(1)} %bitcast.8, f32[2,48,512]{2,1,0:T(8,128)S(1)} %bitcast.9, s32[2,256]{1,0:T(2,128)S(1)} %copy-done.3), custom_call_target="tpu_custom_call" | custom-call | flops 2147483648 | bytes 4194304 | tf_op jit(solution)/shard_map/prepare/pallas_call | solution.py:414
  12.8 1.0 %collective-permute-start.5 = (bf16[112,768]{1,0:T(8,128)(2,1)S(1)}, bf16[112,768]{1,0:T(8,128)(2,1)S(1)}, u32[]{:S(2)}, u32[]{:S(2)}) collective-permute-start(bf16[112,768]{1,0:T(8,128)(2,1)S(1)} %copy-done), channel_id=1, source_target_pairs={{0,5},{1,4},{2,7},{3,6},{4,1},{5,0},{6,3},{7,2},{8,13},{9,12},{10,... | collective-permute-start | bytes 516104 | tf_op jit(solution)/shard_map/ppermute | solution.py:657
  13.8 1.9 %collective-permute-start = (bf16[112,768]{1,0:T(8,128)(2,1)S(1)}, bf16[112,768]{1,0:T(8,128)(2,1)S(1)}, u32[]{:S(2)}, u32[]{:S(2)}) collective-permute-start(bf16[112,768]{1,0:T(8,128)(2,1)S(1)} %copy-done), channel_id=1, source_target_pairs={{0,4},{1,5},{2,6},{3,7},{4,0},{5,1},{6,2},{7,3},{8,12},{9,13},{10,... | collective-permute-start | bytes 516104 | tf_op jit(solution)/shard_map/ppermute | solution.py:657
  15.7 0.0 collective-permute-done.3.refs_3_
  15.7 1.5 %collective-permute-start.4 = (bf16[112,768]{1,0:T(8,128)(2,1)S(1)}, bf16[112,768]{1,0:T(8,128)(2,1)S(1)}, u32[]{:S(2)}, u32[]{:S(2)}) collective-permute-start(bf16[112,768]{1,0:T(8,128)(2,1)S(1)} %collective-permute-done.3.refs_3_), channel_id=1, source_target_pairs={{0,1},{1,0},{2,3},{3,2},{4,5},{5,4},{6,7},{7,6},{8,9},{9,8},{10,11... | collective-permute-start | bytes 516104 | tf_op jit(solution)/shard_map/ppermute | solution.py:657
  17.2 0.9 collective-permute-done.1.refs_2_
  18.1 0.5 collective-permute-start.2
  18.6 0.0 collective-permute-done.6.refs_1_
  18.6 19.0 %layer_sum.2.refs_7_ = f32[2,1024,512]{2,1,0:T(8,128)S(1)} custom-call(bf16[112,768]{1,0:T(8,128)(2,1)S(1)} %copy-done, bf16[112,768]{1,0:T(8,128)(2,1)S(1)} %collective-permute-done.6.refs_1_, bf16[112,768]{1,0:T(8,128)(2,1)S(1)} %collective-permute-done.1.refs_2_, bf16[112,768]{1,0:T(8,128)(2,1)S(1)} %collective-permute-done.3.refs_3_, ...), custom_call_target="tpu_custom_call" | custom-call | flops 9663676416 | bytes 8388608 | tf_op jit(solution)/shard_map/layer_sum/pallas_call | solution.py:455
  37.7 0.0 collective-permute-done.5.refs_3_
  37.7 0.0 collective-permute-done.4.refs_2_
  37.7 0.0 collective-permute-done.2.refs_1_
  37.7 19.7 %layer_sum.3.own = bf16[4,512,512]{2,1,0:T(8,128)(2,1)S(1)} custom-call(bf16[112,768]{1,0:T(8,128)(2,1)S(1)} %collective-permute-done.refs_0_, bf16[112,768]{1,0:T(8,128)(2,1)S(1)} %collective-permute-done.2.refs_1_, bf16[112,768]{1,0:T(8,128)(2,1)S(1)} %collective-permute-done.4.refs_2_, bf16[112,768]{1,0:T(8,128)(2,1)S(1)} %collective-permute-done.5.refs_3_, ...), custom_call_target="tpu_custom_call" | custom-call | flops 9663676416 | bytes 8388608 | tf_op jit(solution)/shard_map/layer_sum/pallas_call | solution.py:455
  57.4 0.1 collective-permute-start.7
  57.5 0.1 stack.23.place
  57.6 4.2 %collective-permute-done.7.other = bf16[4,512,512]{2,1,0:T(8,128)(2,1)} collective-permute-done((bf16[4,512,512]{2,1,0:T(8,128)(2,1)S(1)}, bf16[4,512,512]{2,1,0:T(8,128)(2,1)}, u32[]{:S(2)}, u32[]{:S(2)}) %collective-permute-start.7) | collective-permute-done | bytes 2097184 | tf_op jit(solution)/shard_map/ppermute | solution.py:670
  61.8 4.8 %back.1 = (bf16[2,512,256]{2,1,0:T(8,128)(2,1)S(1)}, bf16[2,256,256]{2,1,0:T(8,128)(2,1)S(1)}) custom-call(s32[5]{0:T(128)S(1)} %stack.23.place, bf16[4,512,512]{2,1,0:T(8,128)(2,1)S(1)} %layer_sum.3.own, bf16[4,512,512]{2,1,0:T(8,128)(2,1)} %collective-permute-done.7.other), custom_call_target="tpu_custom_call" | custom-call | flops 4294967296 | bytes 8388608 | tf_op jit(solution)/shard_map/back/pallas_call | solution.py:540
  66.6 1.7 %collective-permute-start.9 = (bf16[2,256,256]{2,1,0:T(8,128)(2,1)S(1)}, bf16[2,256,256]{2,1,0:T(8,128)(2,1)S(1)}, u32[]{:S(2)}, u32[]{:S(2)}) collective-permute-start(bf16[2,256,256]{2,1,0:T(8,128)(2,1)S(1)} %get-tuple-element.19), channel_id=1, source_target_pairs={{0,16},{8,24},{16,0},{24,8},{1,17},{9,25},{17,1},{25,9},{2,18},{10... | collective-permute-start | bytes 786440 | tf_op jit(solution)/shard_map/ppermute | solution.py:679
  68.3 5.5 %rows.1 = (bf16[2,832,128]{2,1,0:T(8,128)(2,1)S(1)}, bf16[2,832,128]{2,1,0:T(8,128)(2,1)S(1)}) custom-call(s32[5]{0:T(128)S(1)} %stack.23.place, bf16[4,512,512]{2,1,0:T(8,128)(2,1)S(1)} %layer_sum.3.own, bf16[4,512,512]{2,1,0:T(8,128)(2,1)} %collective-permute-done.7.other, bf16[2,512,256]{2,1,0:T(8,128)(2,1)S(1)} %get-tuple-element.18.after.s_mine), custom_call_target="tpu_custom_call" | custom-call | flops 4294967296 | bytes 8388608 | tf_op jit(solution)/shard_map/rows/pallas_call | solution.py:554
  73.8 1.3 %collective-permute-done.9.q_0 = bf16[2,256,256]{2,1,0:T(8,128)(2,1)S(1)} collective-permute-done((bf16[2,256,256]{2,1,0:T(8,128)(2,1)S(1)}, bf16[2,256,256]{2,1,0:T(8,128)(2,1)S(1)}, u32[]{:S(2)}, u32[]{:S(2)}) %collective-permute-start.9) | collective-permute-done | bytes 262176 | tf_op jit(solution)/shard_map/ppermute | solution.py:679
  75.1 1.5 %collective-permute-start.10 = (bf16[2,256,256]{2,1,0:T(8,128)(2,1)S(1)}, bf16[2,256,256]{2,1,0:T(8,128)(2,1)S(1)}, u32[]{:S(2)}, u32[]{:S(2)}) collective-permute-start(bf16[2,256,256]{2,1,0:T(8,128)(2,1)S(1)} %collective-permute-done.9.q_0), channel_id=1, source_target_pairs={{0,1},{1,0},{2,3},{3,2},{4,5},{5,4},{6,7},{7,6},{8,9},{9,8},{10,11... | collective-permute-start | bytes 786440 | tf_op jit(solution)/shard_map/ppermute | solution.py:657
  76.6 1.3 %collective-permute-start.13 = (bf16[2,832,128]{2,1,0:T(8,128)(2,1)S(1)}, bf16[2,832,128]{2,1,0:T(8,128)(2,1)S(1)}, u32[]{:S(2)}, u32[]{:S(2)}) collective-permute-start(bf16[2,832,128]{2,1,0:T(8,128)(2,1)S(1)} %get-tuple-element.23), channel_id=1, source_target_pairs={{0,16},{8,24},{16,0},{24,8},{1,17},{9,25},{17,1},{25,9},{2,18},{10... | collective-permute-start | bytes 1277960 | tf_op jit(solution)/shard_map/ppermute | solution.py:679
  78.0 0.0 collective-permute-start.11
  78.0 4.8 %collective-permute-done.10.q_1 = bf16[2,256,256]{2,1,0:T(8,128)(2,1)S(1)} collective-permute-done((bf16[2,256,256]{2,1,0:T(8,128)(2,1)S(1)}, bf16[2,256,256]{2,1,0:T(8,128)(2,1)S(1)}, u32[]{:S(2)}, u32[]{:S(2)}) %collective-permute-start.10) | collective-permute-done | bytes 262176 | tf_op jit(solution)/shard_map/ppermute | solution.py:657
  82.8 4.7 %collective-permute-done.13.h_sent = bf16[2,832,128]{2,1,0:T(8,128)(2,1)S(1)} collective-permute-done((bf16[2,832,128]{2,1,0:T(8,128)(2,1)S(1)}, bf16[2,832,128]{2,1,0:T(8,128)(2,1)S(1)}, u32[]{:S(2)}, u32[]{:S(2)}) %collective-permute-start.13) | collective-permute-done | bytes 426016 | tf_op jit(solution)/shard_map/ppermute | solution.py:679
  87.6 3.3 %join.1 = (f32[2,64,128]{2,1,0:T(8,128)}, f32[2,64,128]{2,1,0:T(8,128)}) custom-call(s32[5]{0:T(128)S(1)} %stack.23.place, bf16[2,512,256]{2,1,0:T(8,128)(2,1)S(1)} %get-tuple-element.18.after.s_mine, bf16[2,512,256]{2,1,0:T(8,128)(2,1)S(1)} %collective-permute-done.8.s_side, bf16[2,256,256]{2,1,0:T(8,128)(2,1)S(1)} %collective-permute-done.9.q_0, ...), custom_call_target="tpu_custom_call" | custom-call | flops 1073741824 | bytes 4194304 | tf_op jit(solution)/shard_map/join/pallas_call | solution.py:625
  (14 shorter events, 0.0 us)
Async XLA Ops:
  2.6 16.1 %collective-permute-start.6 = (bf16[112,768]{1,0:T(8,128)(2,1)}, bf16[112,768]{1,0:T(8,128)(2,1)S(1)}, u32[]{:S(2)}, u32[]{:S(2)}) collective-permute-start(bf16[112,768]{1,0:T(8,128)(2,1)} %pack.1.refs_0_), channel_id=1, source_target_pairs={{0,1},{1,0},{2,3},{3,2},{4,5},{5,4},{6,7},{7,6},{8,9},{9,8},{10,11... | collective-permute-start | bytes 516104 | tf_op jit(solution)/shard_map/ppermute | solution.py:657
  5.5 10.2 %collective-permute-start.3 = (bf16[112,768]{1,0:T(8,128)(2,1)}, bf16[112,768]{1,0:T(8,128)(2,1)S(1)}, u32[]{:S(2)}, u32[]{:S(2)}) collective-permute-start(bf16[112,768]{1,0:T(8,128)(2,1)} %pack.1.refs_0_), channel_id=1, source_target_pairs={{0,6},{1,7},{2,0},{3,1},{4,2},{5,3},{6,4},{7,5},{8,14},{9,15},{10,... | collective-permute-start | bytes 516104 | tf_op jit(solution)/shard_map/ppermute | solution.py:657
  9.1 9.0 %collective-permute-start.1 = (bf16[112,768]{1,0:T(8,128)(2,1)}, bf16[112,768]{1,0:T(8,128)(2,1)S(1)}, u32[]{:S(2)}, u32[]{:S(2)}) collective-permute-start(bf16[112,768]{1,0:T(8,128)(2,1)} %pack.1.refs_0_), channel_id=1, source_target_pairs={{0,2},{1,3},{2,4},{3,5},{4,6},{5,7},{6,0},{7,1},{8,10},{9,11},{10,... | collective-permute-start | bytes 516104 | tf_op jit(solution)/shard_map/ppermute | solution.py:657
  9.2 1.0 %copy-start.1 = (f32[1,2,2,48,512]{4,3,2,1,0:T(8,128)S(1)}, f32[1,2,2,48,512]{4,3,2,1,0:T(8,128)}, u32[]{:S(2)}) copy-start(f32[1,2,2,48,512]{4,3,2,1,0:T(8,128)} %param.6) | copy-start | bytes 1179652
  10.1 0.9 %copy-start.2 = (f32[1,2,48,512]{3,2,1,0:T(8,128)S(1)}, f32[1,2,48,512]{3,2,1,0:T(8,128)}, u32[]{:S(2)}) copy-start(f32[1,2,48,512]{3,2,1,0:T(8,128)} %param.7) | copy-start | bytes 589828
  11.1 0.7 copy-start.3
  11.8 1.0 %copy-start = (bf16[112,768]{1,0:T(8,128)(2,1)S(1)}, bf16[112,768]{1,0:T(8,128)(2,1)}, u32[]{:S(2)}) copy-start(bf16[112,768]{1,0:T(8,128)(2,1)} %pack.1.refs_0_) | copy-start | bytes 516100
  12.8 24.9 %collective-permute-start.5 = (bf16[112,768]{1,0:T(8,128)(2,1)S(1)}, bf16[112,768]{1,0:T(8,128)(2,1)S(1)}, u32[]{:S(2)}, u32[]{:S(2)}) collective-permute-start(bf16[112,768]{1,0:T(8,128)(2,1)S(1)} %copy-done), channel_id=1, source_target_pairs={{0,5},{1,4},{2,7},{3,6},{4,1},{5,0},{6,3},{7,2},{8,13},{9,12},{10,... | collective-permute-start | bytes 516104 | tf_op jit(solution)/shard_map/ppermute | solution.py:657
  13.8 23.9 %collective-permute-start = (bf16[112,768]{1,0:T(8,128)(2,1)S(1)}, bf16[112,768]{1,0:T(8,128)(2,1)S(1)}, u32[]{:S(2)}, u32[]{:S(2)}) collective-permute-start(bf16[112,768]{1,0:T(8,128)(2,1)S(1)} %copy-done), channel_id=1, source_target_pairs={{0,4},{1,5},{2,6},{3,7},{4,0},{5,1},{6,2},{7,3},{8,12},{9,13},{10,... | collective-permute-start | bytes 516104 | tf_op jit(solution)/shard_map/ppermute | solution.py:657
  15.7 22.0 %collective-permute-start.4 = (bf16[112,768]{1,0:T(8,128)(2,1)S(1)}, bf16[112,768]{1,0:T(8,128)(2,1)S(1)}, u32[]{:S(2)}, u32[]{:S(2)}) collective-permute-start(bf16[112,768]{1,0:T(8,128)(2,1)S(1)} %collective-permute-done.3.refs_3_), channel_id=1, source_target_pairs={{0,1},{1,0},{2,3},{3,2},{4,5},{5,4},{6,7},{7,6},{8,9},{9,8},{10,11... | collective-permute-start | bytes 516104 | tf_op jit(solution)/shard_map/ppermute | solution.py:657
  18.1 19.6 %collective-permute-start.2 = (bf16[112,768]{1,0:T(8,128)(2,1)S(1)}, bf16[112,768]{1,0:T(8,128)(2,1)S(1)}, u32[]{:S(2)}, u32[]{:S(2)}) collective-permute-start(bf16[112,768]{1,0:T(8,128)(2,1)S(1)} %collective-permute-done.1.refs_2_), channel_id=1, source_target_pairs={{0,1},{1,0},{2,3},{3,2},{4,5},{5,4},{6,7},{7,6},{8,9},{9,8},{10,11... | collective-permute-start | bytes 516104 | tf_op jit(solution)/shard_map/ppermute | solution.py:657
  18.6 19.1 %copy-start.4 = (f32[1,512]{1,0:T(1,128)S(1)}, f32[1,512]{1,0:T(1,128)}, u32[]{:S(2)}) copy-start(f32[1,512]{1,0:T(1,128)} %refs_8_.1) | copy-start | bytes 6148
  57.4 4.4 %collective-permute-start.7 = (bf16[4,512,512]{2,1,0:T(8,128)(2,1)S(1)}, bf16[4,512,512]{2,1,0:T(8,128)(2,1)}, u32[]{:S(2)}, u32[]{:S(2)}) collective-permute-start(bf16[4,512,512]{2,1,0:T(8,128)(2,1)S(1)} %layer_sum.3.own), channel_id=1, source_target_pairs={{0,8},{8,0},{16,24},{24,16},{1,9},{9,1},{17,25},{25,17},{2,10},{10... | collective-permute-start | bytes 6291464 | tf_op jit(solution)/shard_map/ppermute | solution.py:670
  66.6 8.5 %collective-permute-start.9 = (bf16[2,256,256]{2,1,0:T(8,128)(2,1)S(1)}, bf16[2,256,256]{2,1,0:T(8,128)(2,1)S(1)}, u32[]{:S(2)}, u32[]{:S(2)}) collective-permute-start(bf16[2,256,256]{2,1,0:T(8,128)(2,1)S(1)} %get-tuple-element.19), channel_id=1, source_target_pairs={{0,16},{8,24},{16,0},{24,8},{1,17},{9,25},{17,1},{25,9},{2,18},{10... | collective-permute-start | bytes 786440 | tf_op jit(solution)/shard_map/ppermute | solution.py:679
  68.2 19.3 %collective-permute-start.8 = (bf16[2,512,256]{2,1,0:T(8,128)(2,1)S(1)}, bf16[2,512,256]{2,1,0:T(8,128)(2,1)S(1)}, u32[]{:S(2)}, u32[]{:S(2)}) collective-permute-start(bf16[2,512,256]{2,1,0:T(8,128)(2,1)S(1)} %get-tuple-element.18.after.s_mine), channel_id=1, source_target_pairs={{0,8},{8,0},{16,24},{24,16},{1,9},{9,1},{17,25},{25,17},{2,10},{10... | collective-permute-start | bytes 1572872 | tf_op jit(solution)/shard_map/ppermute | solution.py:679
  75.1 7.7 %collective-permute-start.10 = (bf16[2,256,256]{2,1,0:T(8,128)(2,1)S(1)}, bf16[2,256,256]{2,1,0:T(8,128)(2,1)S(1)}, u32[]{:S(2)}, u32[]{:S(2)}) collective-permute-start(bf16[2,256,256]{2,1,0:T(8,128)(2,1)S(1)} %collective-permute-done.9.q_0), channel_id=1, source_target_pairs={{0,1},{1,0},{2,3},{3,2},{4,5},{5,4},{6,7},{7,6},{8,9},{9,8},{10,11... | collective-permute-start | bytes 786440 | tf_op jit(solution)/shard_map/ppermute | solution.py:657
  76.6 10.9 %collective-permute-start.13 = (bf16[2,832,128]{2,1,0:T(8,128)(2,1)S(1)}, bf16[2,832,128]{2,1,0:T(8,128)(2,1)S(1)}, u32[]{:S(2)}, u32[]{:S(2)}) collective-permute-start(bf16[2,832,128]{2,1,0:T(8,128)(2,1)S(1)} %get-tuple-element.23), channel_id=1, source_target_pairs={{0,16},{8,24},{16,0},{24,8},{1,17},{9,25},{17,1},{25,9},{2,18},{10... | collective-permute-start | bytes 1277960 | tf_op jit(solution)/shard_map/ppermute | solution.py:679
  78.0 9.6 %collective-permute-start.11 = (bf16[2,256,256]{2,1,0:T(8,128)(2,1)S(1)}, bf16[2,256,256]{2,1,0:T(8,128)(2,1)S(1)}, u32[]{:S(2)}, u32[]{:S(2)}) collective-permute-start(bf16[2,256,256]{2,1,0:T(8,128)(2,1)S(1)} %collective-permute-done.9.q_0), channel_id=1, source_target_pairs={{0,8},{8,0},{16,24},{24,16},{1,9},{9,1},{17,25},{25,17},{2,10},{10... | collective-permute-start | bytes 786440 | tf_op jit(solution)/shard_map/ppermute | solution.py:679
  82.8 4.8 %collective-permute-start.12 = (bf16[2,256,256]{2,1,0:T(8,128)(2,1)S(1)}, bf16[2,256,256]{2,1,0:T(8,128)(2,1)S(1)}, u32[]{:S(2)}, u32[]{:S(2)}) collective-permute-start(bf16[2,256,256]{2,1,0:T(8,128)(2,1)S(1)} %collective-permute-done.10.q_1), channel_id=1, source_target_pairs={{0,8},{8,0},{16,24},{24,16},{1,9},{9,1},{17,25},{25,17},{2,10},{10... | collective-permute-start | bytes 786440 | tf_op jit(solution)/shard_map/ppermute | solution.py:679

commit v2 on v1

--- a/solution.py
+++ b/solution.py
@@ -220,7 +220,7 @@
     depth = spheres * multi
     half_width = waves.shape[1]
     width = 2 * half_width
-    lanes = cos_t.shape[0]
+    lanes = max(128, count * spheres)
     parts = 1
     tall = 2 * width // parts
     few, size = spheres // parts, depth // parts
@@ -240,8 +240,8 @@
         at = slice(spheres * index, spheres * (index + 1))
         cos_s[index] = cos_v[:, at].astype(BF16)
         sin_s[index] = sin_v[:, at].astype(BF16)
-    cos_t[...] = cos_v.T
-    sin_t[...] = sin_v.T
+        cos_t[index] = cos_v.T[at, :]
+        sin_t[index] = sin_v.T[at, :]
     row = lax.broadcasted_iota(jnp.int32, (spheres, depth), 0)
     lane = lax.broadcasted_iota(jnp.int32, (spheres, depth), 1)
     inside = (lane >= row * multi) & (lane < row * multi + multi)
@@ -275,9 +275,9 @@
         while done < many:
             k = (piece * many + done) // multi
             stop = min((k + 1) * multi - piece * many, many)
-            at = spheres * index + part * few + k
-            c = cos_t[pl.ds(at, 1), :]
-            s = sin_t[pl.ds(at, 1), :]
+            at = part * few + k
+            c = cos_t[index, at : at + 1, :]
+            s = sin_t[index, at : at + 1, :]
             to = pl.ds(base + done, stop - done)
             for pol in range(2):
                 lo = pol * half_width
@@ -311,15 +311,17 @@
 
     for task in tasks_of(left_slots[0], spread_slots[0], right_slots[0], 0, 0):
         task()
-    @pl.loop(0, count // 2)
-    def _(pair):
+    for pair in range(count // 2):
         for now in range(2):
             later = 1 - now
             index = 2 * pair + now
-            after = jnp.minimum(index + 1, count - 1)
-            tasks = tasks_of(left_slots[later], spread_slots[later], right_slots[later], after, 0)
-            after = jnp.minimum(index + 2, count - 1)
-            tasks.append(functools.partial(spread, spread_slots[now], after, 0, half_width))
+            after = index + 1
+            tasks = []
+            if after < count:
+              tasks = tasks_of(left_slots[later], spread_slots[later], right_slots[later], after, 0)
+            after = index + 2
+            if after < count:
+              tasks.append(functools.partial(spread, spread_slots[now], after, 0, half_width))
             pieces = [
                 (total, left, right, slice(lane * 256, (lane + 1) * 256))
                 for total, left, right in zip(
@@ -329,9 +331,8 @@
             ]
             for at, (total, left, right, cols) in enumerate(pieces):
                 before = total[:, cols]
-                if now == 0:
-                    before = jnp.where(pair > 0, before, 0.0)
-                total[:, cols] = before + mm(left[...], right[:, cols])
+                product = mm(left[...], right[:, cols])
+                total[:, cols] = product if index == 0 else before + product
                 share = -(-len(tasks) // (len(pieces) - at))
                 for task in tasks[:share]:
                     task()
@@ -432,7 +433,6 @@
     depth = spheres * multi
     half_width = waves.shape[1]
     width = 2 * half_width
-    lanes = max(128, count * spheres)
     operands = list(blocks) + [out_tile, in_pair, waves]
     specs = [ANY] * count + [VMEM] * 3
     if last:
@@ -442,7 +442,7 @@
     else:
         shape = jax.ShapeDtypeStruct((2, 2 * width, width), F32)
     scratch = [pltpu.VMEM((2 * width, width), F32)] * 3
-    scratch += [pltpu.VMEM((lanes, half_width), F32)] * 2
+    scratch += [pltpu.VMEM((count, spheres, half_width), F32)] * 2
     scratch += [pltpu.VMEM((2 * width, depth), BF16)] * 6
     scratch += [pltpu.VMEM((depth, width), BF16)] * 6
     scratch += [pltpu.VMEM((half_width, depth), BF16)] * 4

time: 91.3 us -> 85.3 us (0.934)
  Pallas kernels: 55.3 us -> 49.2 us
    pallas_call x2, Pallas kernels: 38.7 us -> 32.6 us  [layer_sum(): pl.pallas_call(functools.partial(layer_kernel, count, spheres, multi, las...]
  transfers between devices with their start and end apart: 14 -> 14, of which waited for: 5 -> 5; matrix products, arithmetic and copies ran while one was open for 0% -> 0% of each run, Pallas kernels for 28% -> 26%
where the time goes in v2:
time: 85.3 us; the launch traced here: 85 us
  Pallas kernels  49.2 us (58%)
  starting transfers between devices  16.2 us (19%)
  waiting for transfers between devices  15.9 us (19%)
  local copies, waits for them, and re-layouts  2.7 us (3%)
  between operations  0.95 us (1%)
    pallas_call x2, Pallas kernels, layer_sum(): pl.pallas_call(functools.partial(layer_kernel, count, spheres, multi, las...  32.6 us
    ppermute x8, starting transfers between devices, shifted(): return lax.ppermute(value, 'sph', pairs)  13 us
    ppermute x5, waiting for transfers between devices, crossed(): return lax.ppermute(value, 'layer', [(at, at ^ bit) for at in range(4)])  6.08 us
    ppermute x8, waiting for transfers between devices, shifted(): return lax.ppermute(value, 'sph', pairs)  5.7 us
    pallas_call x1, Pallas kernels, form(): pl.pallas_call(functools.partial(rows_kernel, rows), out_shape=(shape, sh...  5.52 us
    pallas_call x1, Pallas kernels, form(): pl.pallas_call(back_kernel, out_shape=(jax.ShapeDtypeStruct((2, width, wi...  4.77 us
    ppermute x1, waiting for transfers between devices, whole_layers(): other = lax.ppermute(own, 'layer', [(at, at ^ 1) for at in range(4)])  4.16 us
    pallas_call x1, Pallas kernels, join(): pl.pallas_call(functools.partial(join_kernel, rows), out_shape=(shape, sh...  3.33 us
  transfers between devices with their start and end apart: 14, of which 5 were waited for; matrix products, arithmetic and copies ran while one was open for 0% of the time, Pallas kernels for 26%

profile of v2, /device:TPU:0, one launch (start us, length us, event | category | flops | bytes accessed | tf_op | source)
XLA Modules:
  0.0 85.0 jit_solution(11624269372171328396)
XLA Ops:
  0.6 1.9 %pack.1.refs_0_ = bf16[112,768]{1,0:T(8,128)(2,1)} custom-call(f32[16,2,48,48]{3,2,1,0:T(8,128)} %bitcast.10, s32[1,16]{1,0:T(1,128)} %sites.1), custom_call_target="tpu_custom_call" | custom-call | tf_op jit(solution)/shard_map/pack/pallas_call | solution.py:384
  2.6 3.0 %collective-permute-start.6 = (bf16[112,768]{1,0:T(8,128)(2,1)}, bf16[112,768]{1,0:T(8,128)(2,1)S(1)}, u32[]{:S(2)}, u32[]{:S(2)}) collective-permute-start(bf16[112,768]{1,0:T(8,128)(2,1)} %pack.1.refs_0_), channel_id=1, source_target_pairs={{0,1},{1,0},{2,3},{3,2},{4,5},{5,4},{6,7},{7,6},{8,9},{9,8},{10,11... | collective-permute-start | bytes 516104 | tf_op jit(solution)/shard_map/ppermute | solution.py:657
  5.5 3.6 %collective-permute-start.3 = (bf16[112,768]{1,0:T(8,128)(2,1)}, bf16[112,768]{1,0:T(8,128)(2,1)S(1)}, u32[]{:S(2)}, u32[]{:S(2)}) collective-permute-start(bf16[112,768]{1,0:T(8,128)(2,1)} %pack.1.refs_0_), channel_id=1, source_target_pairs={{0,6},{1,7},{2,0},{3,1},{4,2},{5,3},{6,4},{7,5},{8,14},{9,15},{10,... | collective-permute-start | bytes 516104 | tf_op jit(solution)/shard_map/ppermute | solution.py:657
  9.1 0.0 collective-permute-start.1
  9.2 1.0 %copy-done.1 = f32[1,2,2,48,512]{4,3,2,1,0:T(8,128)S(1)} copy-done((f32[1,2,2,48,512]{4,3,2,1,0:T(8,128)S(1)}, f32[1,2,2,48,512]{4,3,2,1,0:T(8,128)}, u32[]{:S(2)}) %copy-start.1) | copy-done | bytes 393240
  10.2 0.9 %copy-done.2 = f32[1,2,48,512]{3,2,1,0:T(8,128)S(1)} copy-done((f32[1,2,48,512]{3,2,1,0:T(8,128)S(1)}, f32[1,2,48,512]{3,2,1,0:T(8,128)}, u32[]{:S(2)}) %copy-start.2) | copy-done | bytes 196632
  11.1 0.7 copy-done.3
  11.8 1.0 %prepare.1 = (bf16[2,1024,768]{2,1,0:T(8,128)(2,1)S(1)}, bf16[96,1024]{1,0:T(8,128)(2,1)S(1)}, bf16[16,256]{1,0:T(8,128)(2,1)S(1)}) custom-call(f32[2,2,48,512]{3,2,1,0:T(8,128)S(1)} %bitcast.8, f32[2,48,512]{2,1,0:T(8,128)S(1)} %bitcast.9, s32[2,256]{1,0:T(2,128)S(1)} %copy-done.3), custom_call_target="tpu_custom_call" | custom-call | flops 2147483648 | bytes 4194304 | tf_op jit(solution)/shard_map/prepare/pallas_call | solution.py:415
  12.8 1.0 %collective-permute-start.5 = (bf16[112,768]{1,0:T(8,128)(2,1)S(1)}, bf16[112,768]{1,0:T(8,128)(2,1)S(1)}, u32[]{:S(2)}, u32[]{:S(2)}) collective-permute-start(bf16[112,768]{1,0:T(8,128)(2,1)S(1)} %copy-done), channel_id=1, source_target_pairs={{0,5},{1,4},{2,7},{3,6},{4,1},{5,0},{6,3},{7,2},{8,13},{9,12},{10,... | collective-permute-start | bytes 516104 | tf_op jit(solution)/shard_map/ppermute | solution.py:657
  13.8 1.9 %collective-permute-start = (bf16[112,768]{1,0:T(8,128)(2,1)S(1)}, bf16[112,768]{1,0:T(8,128)(2,1)S(1)}, u32[]{:S(2)}, u32[]{:S(2)}) collective-permute-start(bf16[112,768]{1,0:T(8,128)(2,1)S(1)} %copy-done), channel_id=1, source_target_pairs={{0,4},{1,5},{2,6},{3,7},{4,0},{5,1},{6,2},{7,3},{8,12},{9,13},{10,... | collective-permute-start | bytes 516104 | tf_op jit(solution)/shard_map/ppermute | solution.py:657
  15.7 0.0 collective-permute-done.3.refs_3_
  15.7 1.5 %collective-permute-start.4 = (bf16[112,768]{1,0:T(8,128)(2,1)S(1)}, bf16[112,768]{1,0:T(8,128)(2,1)S(1)}, u32[]{:S(2)}, u32[]{:S(2)}) collective-permute-start(bf16[112,768]{1,0:T(8,128)(2,1)S(1)} %collective-permute-done.3.refs_3_), channel_id=1, source_target_pairs={{0,1},{1,0},{2,3},{3,2},{4,5},{5,4},{6,7},{7,6},{8,9},{9,8},{10,11... | collective-permute-start | bytes 516104 | tf_op jit(solution)/shard_map/ppermute | solution.py:657
  17.2 0.9 %collective-permute-done.1.refs_2_ = bf16[112,768]{1,0:T(8,128)(2,1)S(1)} collective-permute-done((bf16[112,768]{1,0:T(8,128)(2,1)}, bf16[112,768]{1,0:T(8,128)(2,1)S(1)}, u32[]{:S(2)}, u32[]{:S(2)}) %collective-permute-start.1) | collective-permute-done | bytes 172064 | tf_op jit(solution)/shard_map/ppermute | solution.py:657
  18.1 0.5 collective-permute-start.2
  18.6 0.0 collective-permute-done.6.refs_1_
  18.6 16.0 %layer_sum.2.refs_7_ = f32[2,1024,512]{2,1,0:T(8,128)S(1)} custom-call(bf16[112,768]{1,0:T(8,128)(2,1)S(1)} %copy-done, bf16[112,768]{1,0:T(8,128)(2,1)S(1)} %collective-permute-done.6.refs_1_, bf16[112,768]{1,0:T(8,128)(2,1)S(1)} %collective-permute-done.1.refs_2_, bf16[112,768]{1,0:T(8,128)(2,1)S(1)} %collective-permute-done.3.refs_3_, ...), custom_call_target="tpu_custom_call" | custom-call | flops 9663676416 | bytes 8388608 | tf_op jit(solution)/shard_map/layer_sum/pallas_call | solution.py:455
  34.6 0.0 collective-permute-done.refs_0_
  34.7 0.0 collective-permute-done.4.refs_2_
  34.7 16.6 %layer_sum.3.own = bf16[4,512,512]{2,1,0:T(8,128)(2,1)S(1)} custom-call(bf16[112,768]{1,0:T(8,128)(2,1)S(1)} %collective-permute-done.refs_0_, bf16[112,768]{1,0:T(8,128)(2,1)S(1)} %collective-permute-done.2.refs_1_, bf16[112,768]{1,0:T(8,128)(2,1)S(1)} %collective-permute-done.4.refs_2_, bf16[112,768]{1,0:T(8,128)(2,1)S(1)} %collective-permute-done.5.refs_3_, ...), custom_call_target="tpu_custom_call" | custom-call | flops 9663676416 | bytes 8388608 | tf_op jit(solution)/shard_map/layer_sum/pallas_call | solution.py:455
  51.3 0.1 collective-permute-start.7
  51.4 0.1 stack.23.place
  51.5 4.2 %collective-permute-done.7.other = bf16[4,512,512]{2,1,0:T(8,128)(2,1)} collective-permute-done((bf16[4,512,512]{2,1,0:T(8,128)(2,1)S(1)}, bf16[4,512,512]{2,1,0:T(8,128)(2,1)}, u32[]{:S(2)}, u32[]{:S(2)}) %collective-permute-start.7) | collective-permute-done | bytes 2097184 | tf_op jit(solution)/shard_map/ppermute | solution.py:670
  55.7 4.8 %back.1 = (bf16[2,512,256]{2,1,0:T(8,128)(2,1)S(1)}, bf16[2,256,256]{2,1,0:T(8,128)(2,1)S(1)}) custom-call(s32[5]{0:T(128)S(1)} %stack.23.place, bf16[4,512,512]{2,1,0:T(8,128)(2,1)S(1)} %layer_sum.3.own, bf16[4,512,512]{2,1,0:T(8,128)(2,1)} %collective-permute-done.7.other), custom_call_target="tpu_custom_call" | custom-call | flops 4294967296 | bytes 8388608 | tf_op jit(solution)/shard_map/back/pallas_call | solution.py:540
  60.5 1.7 %collective-permute-start.9 = (bf16[2,256,256]{2,1,0:T(8,128)(2,1)S(1)}, bf16[2,256,256]{2,1,0:T(8,128)(2,1)S(1)}, u32[]{:S(2)}, u32[]{:S(2)}) collective-permute-start(bf16[2,256,256]{2,1,0:T(8,128)(2,1)S(1)} %get-tuple-element.19), channel_id=1, source_target_pairs={{0,16},{8,24},{16,0},{24,8},{1,17},{9,25},{17,1},{25,9},{2,18},{10... | collective-permute-start | bytes 786440 | tf_op jit(solution)/shard_map/ppermute | solution.py:679
  62.1 0.0 collective-permute-start.8
  62.2 5.5 %rows.1 = (bf16[2,832,128]{2,1,0:T(8,128)(2,1)S(1)}, bf16[2,832,128]{2,1,0:T(8,128)(2,1)S(1)}) custom-call(s32[5]{0:T(128)S(1)} %stack.23.place, bf16[4,512,512]{2,1,0:T(8,128)(2,1)S(1)} %layer_sum.3.own, bf16[4,512,512]{2,1,0:T(8,128)(2,1)} %collective-permute-done.7.other, bf16[2,512,256]{2,1,0:T(8,128)(2,1)S(1)} %get-tuple-element.18.after.s_mine), custom_call_target="tpu_custom_call" | custom-call | flops 4294967296 | bytes 8388608 | tf_op jit(solution)/shard_map/rows/pallas_call | solution.py:554
  67.7 1.3 %collective-permute-done.9.q_0 = bf16[2,256,256]{2,1,0:T(8,128)(2,1)S(1)} collective-permute-done((bf16[2,256,256]{2,1,0:T(8,128)(2,1)S(1)}, bf16[2,256,256]{2,1,0:T(8,128)(2,1)S(1)}, u32[]{:S(2)}, u32[]{:S(2)}) %collective-permute-start.9) | collective-permute-done | bytes 262176 | tf_op jit(solution)/shard_map/ppermute | solution.py:679
  69.0 1.5 %collective-permute-start.10 = (bf16[2,256,256]{2,1,0:T(8,128)(2,1)S(1)}, bf16[2,256,256]{2,1,0:T(8,128)(2,1)S(1)}, u32[]{:S(2)}, u32[]{:S(2)}) collective-permute-start(bf16[2,256,256]{2,1,0:T(8,128)(2,1)S(1)} %collective-permute-done.9.q_0), channel_id=1, source_target_pairs={{0,1},{1,0},{2,3},{3,2},{4,5},{5,4},{6,7},{7,6},{8,9},{9,8},{10,11... | collective-permute-start | bytes 786440 | tf_op jit(solution)/shard_map/ppermute | solution.py:657
  70.5 1.4 %collective-permute-start.13 = (bf16[2,832,128]{2,1,0:T(8,128)(2,1)S(1)}, bf16[2,832,128]{2,1,0:T(8,128)(2,1)S(1)}, u32[]{:S(2)}, u32[]{:S(2)}) collective-permute-start(bf16[2,832,128]{2,1,0:T(8,128)(2,1)S(1)} %get-tuple-element.23), channel_id=1, source_target_pairs={{0,16},{8,24},{16,0},{24,8},{1,17},{9,25},{17,1},{25,9},{2,18},{10... | collective-permute-start | bytes 1277960 | tf_op jit(solution)/shard_map/ppermute | solution.py:679
  71.9 4.8 %collective-permute-done.10.q_1 = bf16[2,256,256]{2,1,0:T(8,128)(2,1)S(1)} collective-permute-done((bf16[2,256,256]{2,1,0:T(8,128)(2,1)S(1)}, bf16[2,256,256]{2,1,0:T(8,128)(2,1)S(1)}, u32[]{:S(2)}, u32[]{:S(2)}) %collective-permute-start.10) | collective-permute-done | bytes 262176 | tf_op jit(solution)/shard_map/ppermute | solution.py:657
  76.7 4.7 %collective-permute-done.13.h_sent = bf16[2,832,128]{2,1,0:T(8,128)(2,1)S(1)} collective-permute-done((bf16[2,832,128]{2,1,0:T(8,128)(2,1)S(1)}, bf16[2,832,128]{2,1,0:T(8,128)(2,1)S(1)}, u32[]{:S(2)}, u32[]{:S(2)}) %collective-permute-start.13) | collective-permute-done | bytes 426016 | tf_op jit(solution)/shard_map/ppermute | solution.py:679
  81.5 3.3 %join.1 = (f32[2,64,128]{2,1,0:T(8,128)}, f32[2,64,128]{2,1,0:T(8,128)}) custom-call(s32[5]{0:T(128)S(1)} %stack.23.place, bf16[2,512,256]{2,1,0:T(8,128)(2,1)S(1)} %get-tuple-element.18.after.s_mine, bf16[2,512,256]{2,1,0:T(8,128)(2,1)S(1)} %collective-permute-done.8.s_side, bf16[2,256,256]{2,1,0:T(8,128)(2,1)S(1)} %collective-permute-done.9.q_0, ...), custom_call_target="tpu_custom_call" | custom-call | flops 1073741824 | bytes 4194304 | tf_op jit(solution)/shard_map/join/pallas_call | solution.py:625
  (14 shorter events, 0.0 us)
Async XLA Ops:
  2.6 16.1 %collective-permute-start.6 = (bf16[112,768]{1,0:T(8,128)(2,1)}, bf16[112,768]{1,0:T(8,128)(2,1)S(1)}, u32[]{:S(2)}, u32[]{:S(2)}) collective-permute-start(bf16[112,768]{1,0:T(8,128)(2,1)} %pack.1.refs_0_), channel_id=1, source_target_pairs={{0,1},{1,0},{2,3},{3,2},{4,5},{5,4},{6,7},{7,6},{8,9},{9,8},{10,11... | collective-permute-start | bytes 516104 | tf_op jit(solution)/shard_map/ppermute | solution.py:657
  5.5 10.2 %collective-permute-start.3 = (bf16[112,768]{1,0:T(8,128)(2,1)}, bf16[112,768]{1,0:T(8,128)(2,1)S(1)}, u32[]{:S(2)}, u32[]{:S(2)}) collective-permute-start(bf16[112,768]{1,0:T(8,128)(2,1)} %pack.1.refs_0_), channel_id=1, source_target_pairs={{0,6},{1,7},{2,0},{3,1},{4,2},{5,3},{6,4},{7,5},{8,14},{9,15},{10,... | collective-permute-start | bytes 516104 | tf_op jit(solution)/shard_map/ppermute | solution.py:657
  9.1 9.0 %collective-permute-start.1 = (bf16[112,768]{1,0:T(8,128)(2,1)}, bf16[112,768]{1,0:T(8,128)(2,1)S(1)}, u32[]{:S(2)}, u32[]{:S(2)}) collective-permute-start(bf16[112,768]{1,0:T(8,128)(2,1)} %pack.1.refs_0_), channel_id=1, source_target_pairs={{0,2},{1,3},{2,4},{3,5},{4,6},{5,7},{6,0},{7,1},{8,10},{9,11},{10,... | collective-permute-start | bytes 516104 | tf_op jit(solution)/shard_map/ppermute | solution.py:657
  9.2 1.0 %copy-start.1 = (f32[1,2,2,48,512]{4,3,2,1,0:T(8,128)S(1)}, f32[1,2,2,48,512]{4,3,2,1,0:T(8,128)}, u32[]{:S(2)}) copy-start(f32[1,2,2,48,512]{4,3,2,1,0:T(8,128)} %param.6) | copy-start | bytes 1179652
  10.1 0.9 %copy-start.2 = (f32[1,2,48,512]{3,2,1,0:T(8,128)S(1)}, f32[1,2,48,512]{3,2,1,0:T(8,128)}, u32[]{:S(2)}) copy-start(f32[1,2,48,512]{3,2,1,0:T(8,128)} %param.7) | copy-start | bytes 589828
  11.1 0.7 copy-start.3
  11.8 1.0 %copy-start = (bf16[112,768]{1,0:T(8,128)(2,1)S(1)}, bf16[112,768]{1,0:T(8,128)(2,1)}, u32[]{:S(2)}) copy-start(bf16[112,768]{1,0:T(8,128)(2,1)} %pack.1.refs_0_) | copy-start | bytes 516100
  12.8 21.9 %collective-permute-start.5 = (bf16[112,768]{1,0:T(8,128)(2,1)S(1)}, bf16[112,768]{1,0:T(8,128)(2,1)S(1)}, u32[]{:S(2)}, u32[]{:S(2)}) collective-permute-start(bf16[112,768]{1,0:T(8,128)(2,1)S(1)} %copy-done), channel_id=1, source_target_pairs={{0,5},{1,4},{2,7},{3,6},{4,1},{5,0},{6,3},{7,2},{8,13},{9,12},{10,... | collective-permute-start | bytes 516104 | tf_op jit(solution)/shard_map/ppermute | solution.py:657
  13.8 20.8 %collective-permute-start = (bf16[112,768]{1,0:T(8,128)(2,1)S(1)}, bf16[112,768]{1,0:T(8,128)(2,1)S(1)}, u32[]{:S(2)}, u32[]{:S(2)}) collective-permute-start(bf16[112,768]{1,0:T(8,128)(2,1)S(1)} %copy-done), channel_id=1, source_target_pairs={{0,4},{1,5},{2,6},{3,7},{4,0},{5,1},{6,2},{7,3},{8,12},{9,13},{10,... | collective-permute-start | bytes 516104 | tf_op jit(solution)/shard_map/ppermute | solution.py:657
  15.7 18.9 %collective-permute-start.4 = (bf16[112,768]{1,0:T(8,128)(2,1)S(1)}, bf16[112,768]{1,0:T(8,128)(2,1)S(1)}, u32[]{:S(2)}, u32[]{:S(2)}) collective-permute-start(bf16[112,768]{1,0:T(8,128)(2,1)S(1)} %collective-permute-done.3.refs_3_), channel_id=1, source_target_pairs={{0,1},{1,0},{2,3},{3,2},{4,5},{5,4},{6,7},{7,6},{8,9},{9,8},{10,11... | collective-permute-start | bytes 516104 | tf_op jit(solution)/shard_map/ppermute | solution.py:657
  18.1 16.5 %collective-permute-start.2 = (bf16[112,768]{1,0:T(8,128)(2,1)S(1)}, bf16[112,768]{1,0:T(8,128)(2,1)S(1)}, u32[]{:S(2)}, u32[]{:S(2)}) collective-permute-start(bf16[112,768]{1,0:T(8,128)(2,1)S(1)} %collective-permute-done.1.refs_2_), channel_id=1, source_target_pairs={{0,1},{1,0},{2,3},{3,2},{4,5},{5,4},{6,7},{7,6},{8,9},{9,8},{10,11... | collective-permute-start | bytes 516104 | tf_op jit(solution)/shard_map/ppermute | solution.py:657
  18.6 16.0 %copy-start.4 = (f32[1,512]{1,0:T(1,128)S(1)}, f32[1,512]{1,0:T(1,128)}, u32[]{:S(2)}) copy-start(f32[1,512]{1,0:T(1,128)} %refs_8_.1) | copy-start | bytes 6148
  51.3 4.4 %collective-permute-start.7 = (bf16[4,512,512]{2,1,0:T(8,128)(2,1)S(1)}, bf16[4,512,512]{2,1,0:T(8,128)(2,1)}, u32[]{:S(2)}, u32[]{:S(2)}) collective-permute-start(bf16[4,512,512]{2,1,0:T(8,128)(2,1)S(1)} %layer_sum.3.own), channel_id=1, source_target_pairs={{0,8},{8,0},{16,24},{24,16},{1,9},{9,1},{17,25},{25,17},{2,10},{10... | collective-permute-start | bytes 6291464 | tf_op jit(solution)/shard_map/ppermute | solution.py:670
  60.5 8.6 %collective-permute-start.9 = (bf16[2,256,256]{2,1,0:T(8,128)(2,1)S(1)}, bf16[2,256,256]{2,1,0:T(8,128)(2,1)S(1)}, u32[]{:S(2)}, u32[]{:S(2)}) collective-permute-start(bf16[2,256,256]{2,1,0:T(8,128)(2,1)S(1)} %get-tuple-element.19), channel_id=1, source_target_pairs={{0,16},{8,24},{16,0},{24,8},{1,17},{9,25},{17,1},{25,9},{2,18},{10... | collective-permute-start | bytes 786440 | tf_op jit(solution)/shard_map/ppermute | solution.py:679
  62.1 19.3 %collective-permute-start.8 = (bf16[2,512,256]{2,1,0:T(8,128)(2,1)S(1)}, bf16[2,512,256]{2,1,0:T(8,128)(2,1)S(1)}, u32[]{:S(2)}, u32[]{:S(2)}) collective-permute-start(bf16[2,512,256]{2,1,0:T(8,128)(2,1)S(1)} %get-tuple-element.18.after.s_mine), channel_id=1, source_target_pairs={{0,8},{8,0},{16,24},{24,16},{1,9},{9,1},{17,25},{25,17},{2,10},{10... | collective-permute-start | bytes 1572872 | tf_op jit(solution)/shard_map/ppermute | solution.py:679
  69.0 7.7 %collective-permute-start.10 = (bf16[2,256,256]{2,1,0:T(8,128)(2,1)S(1)}, bf16[2,256,256]{2,1,0:T(8,128)(2,1)S(1)}, u32[]{:S(2)}, u32[]{:S(2)}) collective-permute-start(bf16[2,256,256]{2,1,0:T(8,128)(2,1)S(1)} %collective-permute-done.9.q_0), channel_id=1, source_target_pairs={{0,1},{1,0},{2,3},{3,2},{4,5},{5,4},{6,7},{7,6},{8,9},{9,8},{10,11... | collective-permute-start | bytes 786440 | tf_op jit(solution)/shard_map/ppermute | solution.py:657
  70.5 10.9 %collective-permute-start.13 = (bf16[2,832,128]{2,1,0:T(8,128)(2,1)S(1)}, bf16[2,832,128]{2,1,0:T(8,128)(2,1)S(1)}, u32[]{:S(2)}, u32[]{:S(2)}) collective-permute-start(bf16[2,832,128]{2,1,0:T(8,128)(2,1)S(1)} %get-tuple-element.23), channel_id=1, source_target_pairs={{0,16},{8,24},{16,0},{24,8},{1,17},{9,25},{17,1},{25,9},{2,18},{10... | collective-permute-start | bytes 1277960 | tf_op jit(solution)/shard_map/ppermute | solution.py:679
  71.9 9.5 %collective-permute-start.11 = (bf16[2,256,256]{2,1,0:T(8,128)(2,1)S(1)}, bf16[2,256,256]{2,1,0:T(8,128)(2,1)S(1)}, u32[]{:S(2)}, u32[]{:S(2)}) collective-permute-start(bf16[2,256,256]{2,1,0:T(8,128)(2,1)S(1)} %collective-permute-done.9.q_0), channel_id=1, source_target_pairs={{0,8},{8,0},{16,24},{24,16},{1,9},{9,1},{17,25},{25,17},{2,10},{10... | collective-permute-start | bytes 786440 | tf_op jit(solution)/shard_map/ppermute | solution.py:679
  76.7 4.8 %collective-permute-start.12 = (bf16[2,256,256]{2,1,0:T(8,128)(2,1)S(1)}, bf16[2,256,256]{2,1,0:T(8,128)(2,1)S(1)}, u32[]{:S(2)}, u32[]{:S(2)}) collective-permute-start(bf16[2,256,256]{2,1,0:T(8,128)(2,1)S(1)} %collective-permute-done.10.q_1), channel_id=1, source_target_pairs={{0,8},{8,0},{16,24},{24,16},{1,9},{9,1},{17,25},{25,17},{2,10},{10... | collective-permute-start | bytes 786440 | tf_op jit(solution)/shard_map/ppermute | solution.py:679

commit v3 on v2

--- a/solution.py
+++ b/solution.py
@@ -228,10 +228,11 @@
     for copy in copies:
         copy.wait()
     coords = None
+    row = lax.broadcasted_iota(jnp.int32, (depth, lanes), 0)
+    lane = lax.broadcasted_iota(jnp.int32, (depth, lanes), 1)
+    lead = row - lane * multi
     for index, block in enumerate(blocks):
-        row = lax.broadcasted_iota(jnp.int32, (depth, lanes), 0)
-        lane = lax.broadcasted_iota(jnp.int32, (depth, lanes), 1)
-        pick = (row == (lane - spheres * index) * multi).astype(F32).astype(BF16)
+        pick = (lead == -depth * index).astype(F32).astype(BF16)
         part = mm(block[2 * multi : 2 * multi + EXTRA, :], pick)
         coords = part if coords is None else coords + part
     turns = mm_t(waves[...], coords.astype(BF16))
@@ -464,31 +465,38 @@
     )(*operands)
 
 
-def take_pair(place, own, other, u, v, sems):
-    def take(to, source, at):
-        return pltpu.make_async_copy(source, to, sems.at[at])
+def take_pair(place, own, other, u, v, sems, order):
+    def take(to, source, side, kind):
+        at = pl.ds(2 * kind, 2)
+        return pltpu.make_async_copy(source.at[at], to.at[at], sems.at[2 * side + kind])
 
     @pl.when(place[0] == 1)
     def _():
-        take(u, own, 0).start()
-        take(v, other, 1).start()
+        for side, kind in order:
+            take((u, v)[side], (own, other)[side], side, kind).start()
 
     @pl.when(place[0] == 0)
     def _():
-        take(u, other, 0).start()
-        take(v, own, 1).start()
-
-    take(u, own, 0).wait()
-    take(v, own, 1).wait()
-    return (u[0], u[1]), (u[2], u[3]), (v[0], v[1]), (v[2], v[3])
+        for side, kind in order:
+            take((u, v)[side], (other, own)[side], side, kind).start()
+
+    def arrived(side, kind):
+        take((u, v)[side], own, side, kind).wait()
+        ref = (u, v)[side]
+        return (ref[2 * kind], ref[2 * kind + 1])
+
+    return arrived
 
 
 def back_kernel(place, own, other, s_out, s_send, u, v, sems):
     side = own.shape[1] // 2
-    r_u, t_u, r_v, _ = take_pair(place, own, other, u, v, sems)
+    arrived = take_pair(place, own, other, u, v, sems, ((0, 1), (1, 0), (0, 0)))
     mine = pl.ds(pl.multiple_of(place[1] * side, side), side)
+    t_u = arrived(0, 1)
+    r_v = arrived(1, 0)
     base = (u[2, :, mine], u[3, :, mine])
     up = cmul(r_v, base)
+    r_u = arrived(0, 0)
     again = cmul(r_u, half(up))
     again = cmul(r_v, half(again))
     up = half(add(up, again))
@@ -503,16 +511,20 @@
     width = own.shape[1]
     quarter = width // 4
     core = place[1]
-    r_u, t_u, r_v, _ = take_pair(place, own, other, u, v, sems)
+    arrived = take_pair(place, own, other, u, v, sems, ((1, 1), (0, 0), (1, 0), (0, 1)))
     near = pl.ds(pl.multiple_of(core * quarter, quarter), quarter)
     far = pl.ds(pl.multiple_of((core + 2) * quarter, quarter), quarter)
 
     def columns(ref, at):
         return jnp.concatenate([ref[at, :, near], ref[at, :, far]], axis=1)
 
+    arrived(1, 1)
     base = (columns(v, 2), columns(v, 3))
+    r_u = arrived(0, 0)
     chain = cmul(r_u, base)
+    r_v = arrived(1, 0)
     chain = cmul(r_v, half(chain))
+    t_u = arrived(0, 1)
     chain = half((base[0] + chain[0], base[1] + chain[1]))
     here = cmul(t_u, chain)
     my = pl.ds(pl.multiple_of(place[2] * rows, rows), rows)
@@ -535,7 +547,7 @@
 
 def form(place, own, other, rows):
     width = own.shape[1]
-    scratch = [pltpu.VMEM(own.shape, BF16)] * 2 + [pltpu.SemaphoreType.DMA((2,))]
+    scratch = [pltpu.VMEM(own.shape, BF16)] * 2 + [pltpu.SemaphoreType.DMA((4,))]
     params = pltpu.CompilerParams(vmem_limit_bytes=24 * 2**20)
     back, send = pl.pallas_call(
         back_kernel,
@@ -573,20 +585,22 @@
     this = pl.ds(pl.multiple_of(place[4] * many, many), many)
     that = pl.ds(pl.multiple_of((1 - place[4]) * many, many), many)
     moves = (
-        (s_mine, sides.at[lower, core]),
-        (s_side, sides.at[lower, 1 - core]),
-        (q_0, sides.at[1 - lower, core, :, this, :]),
-        (q_1, sides.at[1 - lower, core, :, that, :]),
-        (q_2, sides.at[1 - lower, 1 - core, :, this, :]),
-        (q_3, sides.at[1 - lower, 1 - core, :, that, :]),
-        (h_near, h.at[lower]),
-        (h_sent, h.at[1 - lower]),
-    )
-    copies = [pltpu.make_async_copy(*move, sems.at[at]) for at, move in enumerate(moves)]
-    for copy in copies:
-        copy.start()
-    for copy in copies:
-        copy.wait()
+        ((h_near, h.at[lower]), 2),
+        ((h_sent, h.at[1 - lower]), 2),
+        ((s_mine, sides.at[lower, core]), lower),
+        ((s_side, sides.at[lower, 1 - core]), lower),
+        ((q_0, sides.at[1 - lower, core, :, this, :]), 1 - lower),
+        ((q_1, sides.at[1 - lower, core, :, that, :]), 1 - lower),
+        ((q_2, sides.at[1 - lower, 1 - core, :, this, :]), 1 - lower),
+        ((q_3, sides.at[1 - lower, 1 - core, :, that, :]), 1 - lower),
+    )
+    for move, at in moves:
+        pltpu.make_async_copy(*move, sems.at[at]).start()
+
+    def arrived(ref, at):
+        pltpu.make_async_copy(ref, ref, sems.at[at]).wait()
+
+    arrived(h, 2)
 
     def rows_of(side):
         return tuple(
@@ -609,8 +623,10 @@
 
     from_above = rows_of(0)
     from_below = rows_of(1)
+    arrived(sides.at[1], 1)
     second = half(times(from_above, 1))
     both = tuple(jnp.concatenate([from_below[c], second[c]], axis=0) for c in range(2))
+    arrived(sides.at[0], 0)
     chain = times(half(times(both, 0)), 1)
     chain = half(tuple(both[c].astype(F32) + chain[c] for c in range(2)))
     result = cmul(chain, (h[0, 0, 0:width, :], h[0, 1, 0:width, :]))
@@ -630,7 +646,7 @@
         scratch_shapes=[
             pltpu.VMEM((2, 2) + s_mine.shape, BF16),
             pltpu.VMEM((2,) + h_near.shape, BF16),
-            pltpu.SemaphoreType.DMA((8,)),
+            pltpu.SemaphoreType.DMA((3,)),
         ],
         compiler_params=pltpu.CompilerParams(vmem_limit_bytes=20 * 2**20),
         cost_estimate=pl.CostEstimate(flops=2**30, bytes_accessed=2**22, transcendentals=0),

time: 85.3 us -> 85 us (level)
  transfers between devices with their start and end apart: 14 -> 14, of which waited for: 5 -> 5; matrix products, arithmetic and copies ran while one was open for 0% -> 0% of each run, Pallas kernels for 26% -> 27%
where the time goes in v3:
time: 85 us; the launch traced here: 84.7 us
  Pallas kernels  49.3 us (58%)
  starting transfers between devices  16.2 us (19%)
  waiting for transfers between devices  15.6 us (18%)
  local copies, waits for them, and re-layouts  2.7 us (3%)
  between operations  0.95 us (1%)
    pallas_call x2, Pallas kernels, layer_sum(): pl.pallas_call(functools.partial(layer_kernel, count, spheres, multi, las...  32.6 us
    ppermute x8, starting transfers between devices, shifted(): return lax.ppermute(value, 'sph', pairs)  13 us
    ppermute x5, waiting for transfers between devices, crossed(): return lax.ppermute(value, 'layer', [(at, at ^ bit) for at in range(4)])  5.91 us
    pallas_call x1, Pallas kernels, form(): pl.pallas_call(functools.partial(rows_kernel, rows), out_shape=(shape, sh...  5.71 us
    ppermute x8, waiting for transfers between devices, shifted(): return lax.ppermute(value, 'sph', pairs)  5.51 us
    pallas_call x1, Pallas kernels, form(): pl.pallas_call(back_kernel, out_shape=(jax.ShapeDtypeStruct((2, width, wi...  4.58 us
    ppermute x1, waiting for transfers between devices, whole_layers(): other = lax.ppermute(own, 'layer', [(at, at ^ 1) for at in range(4)])  4.16 us
    pallas_call x1, Pallas kernels, join(): pl.pallas_call(functools.partial(join_kernel, rows), out_shape=(shape, sh...  3.44 us
  transfers between devices with their start and end apart: 14, of which 5 were waited for; matrix products, arithmetic and copies ran while one was open for 0% of the time, Pallas kernels for 27%

profile of v3, /device:TPU:0, one launch (start us, length us, event | category | flops | bytes accessed | tf_op | source)
XLA Modules:
  0.0 84.7 jit_solution(14820766619112098457)
XLA Ops:
  0.6 1.9 %pack.1.refs_0_ = bf16[112,768]{1,0:T(8,128)(2,1)} custom-call(f32[16,2,48,48]{3,2,1,0:T(8,128)} %bitcast.10, s32[1,16]{1,0:T(1,128)} %sites.1), custom_call_target="tpu_custom_call" | custom-call | tf_op jit(solution)/shard_map/pack/pallas_call | solution.py:385
  2.6 3.0 %collective-permute-start.6 = (bf16[112,768]{1,0:T(8,128)(2,1)}, bf16[112,768]{1,0:T(8,128)(2,1)S(1)}, u32[]{:S(2)}, u32[]{:S(2)}) collective-permute-start(bf16[112,768]{1,0:T(8,128)(2,1)} %pack.1.refs_0_), channel_id=1, source_target_pairs={{0,1},{1,0},{2,3},{3,2},{4,5},{5,4},{6,7},{7,6},{8,9},{9,8},{10,11... | collective-permute-start | bytes 516104 | tf_op jit(solution)/shard_map/ppermute | solution.py:673
  5.5 3.6 %collective-permute-start.3 = (bf16[112,768]{1,0:T(8,128)(2,1)}, bf16[112,768]{1,0:T(8,128)(2,1)S(1)}, u32[]{:S(2)}, u32[]{:S(2)}) collective-permute-start(bf16[112,768]{1,0:T(8,128)(2,1)} %pack.1.refs_0_), channel_id=1, source_target_pairs={{0,6},{1,7},{2,0},{3,1},{4,2},{5,3},{6,4},{7,5},{8,14},{9,15},{10,... | collective-permute-start | bytes 516104 | tf_op jit(solution)/shard_map/ppermute | solution.py:673
  9.2 1.0 %copy-done.1 = f32[1,2,2,48,512]{4,3,2,1,0:T(8,128)S(1)} copy-done((f32[1,2,2,48,512]{4,3,2,1,0:T(8,128)S(1)}, f32[1,2,2,48,512]{4,3,2,1,0:T(8,128)}, u32[]{:S(2)}) %copy-start.1) | copy-done | bytes 393240
  10.2 0.9 %copy-done.2 = f32[1,2,48,512]{3,2,1,0:T(8,128)S(1)} copy-done((f32[1,2,48,512]{3,2,1,0:T(8,128)S(1)}, f32[1,2,48,512]{3,2,1,0:T(8,128)}, u32[]{:S(2)}) %copy-start.2) | copy-done | bytes 196632
  11.1 0.7 copy-done.3
  11.8 1.0 %prepare.1 = (bf16[2,1024,768]{2,1,0:T(8,128)(2,1)S(1)}, bf16[96,1024]{1,0:T(8,128)(2,1)S(1)}, bf16[16,256]{1,0:T(8,128)(2,1)S(1)}) custom-call(f32[2,2,48,512]{3,2,1,0:T(8,128)S(1)} %bitcast.8, f32[2,48,512]{2,1,0:T(8,128)S(1)} %bitcast.9, s32[2,256]{1,0:T(2,128)S(1)} %copy-done.3), custom_call_target="tpu_custom_call" | custom-call | flops 2147483648 | bytes 4194304 | tf_op jit(solution)/shard_map/prepare/pallas_call | solution.py:416
  12.8 1.0 %collective-permute-start.5 = (bf16[112,768]{1,0:T(8,128)(2,1)S(1)}, bf16[112,768]{1,0:T(8,128)(2,1)S(1)}, u32[]{:S(2)}, u32[]{:S(2)}) collective-permute-start(bf16[112,768]{1,0:T(8,128)(2,1)S(1)} %copy-done), channel_id=1, source_target_pairs={{0,5},{1,4},{2,7},{3,6},{4,1},{5,0},{6,3},{7,2},{8,13},{9,12},{10,... | collective-permute-start | bytes 516104 | tf_op jit(solution)/shard_map/ppermute | solution.py:673
  13.8 1.9 %collective-permute-start = (bf16[112,768]{1,0:T(8,128)(2,1)S(1)}, bf16[112,768]{1,0:T(8,128)(2,1)S(1)}, u32[]{:S(2)}, u32[]{:S(2)}) collective-permute-start(bf16[112,768]{1,0:T(8,128)(2,1)S(1)} %copy-done), channel_id=1, source_target_pairs={{0,4},{1,5},{2,6},{3,7},{4,0},{5,1},{6,2},{7,3},{8,12},{9,13},{10,... | collective-permute-start | bytes 516104 | tf_op jit(solution)/shard_map/ppermute | solution.py:673
  15.7 0.0 collective-permute-done.3.refs_3_
  15.7 1.5 %collective-permute-start.4 = (bf16[112,768]{1,0:T(8,128)(2,1)S(1)}, bf16[112,768]{1,0:T(8,128)(2,1)S(1)}, u32[]{:S(2)}, u32[]{:S(2)}) collective-permute-start(bf16[112,768]{1,0:T(8,128)(2,1)S(1)} %collective-permute-done.3.refs_3_), channel_id=1, source_target_pairs={{0,1},{1,0},{2,3},{3,2},{4,5},{5,4},{6,7},{7,6},{8,9},{9,8},{10,11... | collective-permute-start | bytes 516104 | tf_op jit(solution)/shard_map/ppermute | solution.py:673
  17.2 0.9 %collective-permute-done.1.refs_2_ = bf16[112,768]{1,0:T(8,128)(2,1)S(1)} collective-permute-done((bf16[112,768]{1,0:T(8,128)(2,1)}, bf16[112,768]{1,0:T(8,128)(2,1)S(1)}, u32[]{:S(2)}, u32[]{:S(2)}) %collective-permute-start.1) | collective-permute-done | bytes 172064 | tf_op jit(solution)/shard_map/ppermute | solution.py:673
  18.1 0.5 collective-permute-start.2
  18.6 0.0 collective-permute-done.6.refs_1_
  18.6 16.0 %layer_sum.2.refs_7_ = f32[2,1024,512]{2,1,0:T(8,128)S(1)} custom-call(bf16[112,768]{1,0:T(8,128)(2,1)S(1)} %copy-done, bf16[112,768]{1,0:T(8,128)(2,1)S(1)} %collective-permute-done.6.refs_1_, bf16[112,768]{1,0:T(8,128)(2,1)S(1)} %collective-permute-done.1.refs_2_, bf16[112,768]{1,0:T(8,128)(2,1)S(1)} %collective-permute-done.3.refs_3_, ...), custom_call_target="tpu_custom_call" | custom-call | flops 9663676416 | bytes 8388608 | tf_op jit(solution)/shard_map/layer_sum/pallas_call | solution.py:456
  34.6 0.0 collective-permute-done.refs_0_
  34.6 0.0 collective-permute-done.4.refs_2_
  34.7 16.7 %layer_sum.3.own = bf16[4,512,512]{2,1,0:T(8,128)(2,1)S(1)} custom-call(bf16[112,768]{1,0:T(8,128)(2,1)S(1)} %collective-permute-done.refs_0_, bf16[112,768]{1,0:T(8,128)(2,1)S(1)} %collective-permute-done.2.refs_1_, bf16[112,768]{1,0:T(8,128)(2,1)S(1)} %collective-permute-done.4.refs_2_, bf16[112,768]{1,0:T(8,128)(2,1)S(1)} %collective-permute-done.5.refs_3_, ...), custom_call_target="tpu_custom_call" | custom-call | flops 9663676416 | bytes 8388608 | tf_op jit(solution)/shard_map/layer_sum/pallas_call | solution.py:456
  51.3 0.1 collective-permute-start.7
  51.5 0.1 stack.23.place
  51.5 4.2 %collective-permute-done.7.other = bf16[4,512,512]{2,1,0:T(8,128)(2,1)} collective-permute-done((bf16[4,512,512]{2,1,0:T(8,128)(2,1)S(1)}, bf16[4,512,512]{2,1,0:T(8,128)(2,1)}, u32[]{:S(2)}, u32[]{:S(2)}) %collective-permute-start.7) | collective-permute-done | bytes 2097184 | tf_op jit(solution)/shard_map/ppermute | solution.py:686
  55.7 4.6 %back.1 = (bf16[2,512,256]{2,1,0:T(8,128)(2,1)S(1)}, bf16[2,256,256]{2,1,0:T(8,128)(2,1)S(1)}) custom-call(s32[5]{0:T(128)S(1)} %stack.23.place, bf16[4,512,512]{2,1,0:T(8,128)(2,1)S(1)} %layer_sum.3.own, bf16[4,512,512]{2,1,0:T(8,128)(2,1)} %collective-permute-done.7.other), custom_call_target="tpu_custom_call" | custom-call | flops 4294967296 | bytes 8388608 | tf_op jit(solution)/shard_map/back/pallas_call | solution.py:552
  60.3 1.5 %collective-permute-start.9 = (bf16[2,256,256]{2,1,0:T(8,128)(2,1)S(1)}, bf16[2,256,256]{2,1,0:T(8,128)(2,1)S(1)}, u32[]{:S(2)}, u32[]{:S(2)}) collective-permute-start(bf16[2,256,256]{2,1,0:T(8,128)(2,1)S(1)} %get-tuple-element.19), channel_id=1, source_target_pairs={{0,16},{8,24},{16,0},{24,8},{1,17},{9,25},{17,1},{25,9},{2,18},{10... | collective-permute-start | bytes 786440 | tf_op jit(solution)/shard_map/ppermute | solution.py:695
  61.8 0.0 collective-permute-start.8
  61.8 5.7 %rows.1 = (bf16[2,832,128]{2,1,0:T(8,128)(2,1)S(1)}, bf16[2,832,128]{2,1,0:T(8,128)(2,1)S(1)}) custom-call(s32[5]{0:T(128)S(1)} %stack.23.place, bf16[4,512,512]{2,1,0:T(8,128)(2,1)S(1)} %layer_sum.3.own, bf16[4,512,512]{2,1,0:T(8,128)(2,1)} %collective-permute-done.7.other, bf16[2,512,256]{2,1,0:T(8,128)(2,1)S(1)} %get-tuple-element.18.after.s_mine), custom_call_target="tpu_custom_call" | custom-call | flops 4294967296 | bytes 8388608 | tf_op jit(solution)/shard_map/rows/pallas_call | solution.py:566
  67.6 1.1 %collective-permute-done.9.q_0 = bf16[2,256,256]{2,1,0:T(8,128)(2,1)S(1)} collective-permute-done((bf16[2,256,256]{2,1,0:T(8,128)(2,1)S(1)}, bf16[2,256,256]{2,1,0:T(8,128)(2,1)S(1)}, u32[]{:S(2)}, u32[]{:S(2)}) %collective-permute-start.9) | collective-permute-done | bytes 262176 | tf_op jit(solution)/shard_map/ppermute | solution.py:695
  68.7 1.5 %collective-permute-start.10 = (bf16[2,256,256]{2,1,0:T(8,128)(2,1)S(1)}, bf16[2,256,256]{2,1,0:T(8,128)(2,1)S(1)}, u32[]{:S(2)}, u32[]{:S(2)}) collective-permute-start(bf16[2,256,256]{2,1,0:T(8,128)(2,1)S(1)} %collective-permute-done.9.q_0), channel_id=1, source_target_pairs={{0,1},{1,0},{2,3},{3,2},{4,5},{5,4},{6,7},{7,6},{8,9},{9,8},{10,11... | collective-permute-start | bytes 786440 | tf_op jit(solution)/shard_map/ppermute | solution.py:673
  70.2 1.5 %collective-permute-start.13 = (bf16[2,832,128]{2,1,0:T(8,128)(2,1)S(1)}, bf16[2,832,128]{2,1,0:T(8,128)(2,1)S(1)}, u32[]{:S(2)}, u32[]{:S(2)}) collective-permute-start(bf16[2,832,128]{2,1,0:T(8,128)(2,1)S(1)} %get-tuple-element.23), channel_id=1, source_target_pairs={{0,16},{8,24},{16,0},{24,8},{1,17},{9,25},{17,1},{25,9},{2,18},{10... | collective-permute-start | bytes 1277960 | tf_op jit(solution)/shard_map/ppermute | solution.py:695
  71.7 4.6 %collective-permute-done.10.q_1 = bf16[2,256,256]{2,1,0:T(8,128)(2,1)S(1)} collective-permute-done((bf16[2,256,256]{2,1,0:T(8,128)(2,1)S(1)}, bf16[2,256,256]{2,1,0:T(8,128)(2,1)S(1)}, u32[]{:S(2)}, u32[]{:S(2)}) %collective-permute-start.10) | collective-permute-done | bytes 262176 | tf_op jit(solution)/shard_map/ppermute | solution.py:673
  76.3 4.8 %collective-permute-done.13.h_sent = bf16[2,832,128]{2,1,0:T(8,128)(2,1)S(1)} collective-permute-done((bf16[2,832,128]{2,1,0:T(8,128)(2,1)S(1)}, bf16[2,832,128]{2,1,0:T(8,128)(2,1)S(1)}, u32[]{:S(2)}, u32[]{:S(2)}) %collective-permute-start.13) | collective-permute-done | bytes 426016 | tf_op jit(solution)/shard_map/ppermute | solution.py:695
  81.1 0.0 collective-permute-done.11.q_2
  81.1 3.4 %join.1 = (f32[2,64,128]{2,1,0:T(8,128)}, f32[2,64,128]{2,1,0:T(8,128)}) custom-call(s32[5]{0:T(128)S(1)} %stack.23.place, bf16[2,512,256]{2,1,0:T(8,128)(2,1)S(1)} %get-tuple-element.18.after.s_mine, bf16[2,512,256]{2,1,0:T(8,128)(2,1)S(1)} %collective-permute-done.8.s_side, bf16[2,256,256]{2,1,0:T(8,128)(2,1)S(1)} %collective-permute-done.9.q_0, ...), custom_call_target="tpu_custom_call" | custom-call | flops 1073741824 | bytes 4194304 | tf_op jit(solution)/shard_map/join/pallas_call | solution.py:641
  (14 shorter events, 0.0 us)
Async XLA Ops:
  2.6 16.1 %collective-permute-start.6 = (bf16[112,768]{1,0:T(8,128)(2,1)}, bf16[112,768]{1,0:T(8,128)(2,1)S(1)}, u32[]{:S(2)}, u32[]{:S(2)}) collective-permute-start(bf16[112,768]{1,0:T(8,128)(2,1)} %pack.1.refs_0_), channel_id=1, source_target_pairs={{0,1},{1,0},{2,3},{3,2},{4,5},{5,4},{6,7},{7,6},{8,9},{9,8},{10,11... | collective-permute-start | bytes 516104 | tf_op jit(solution)/shard_map/ppermute | solution.py:673
  5.5 10.2 %collective-permute-start.3 = (bf16[112,768]{1,0:T(8,128)(2,1)}, bf16[112,768]{1,0:T(8,128)(2,1)S(1)}, u32[]{:S(2)}, u32[]{:S(2)}) collective-permute-start(bf16[112,768]{1,0:T(8,128)(2,1)} %pack.1.refs_0_), channel_id=1, source_target_pairs={{0,6},{1,7},{2,0},{3,1},{4,2},{5,3},{6,4},{7,5},{8,14},{9,15},{10,... | collective-permute-start | bytes 516104 | tf_op jit(solution)/shard_map/ppermute | solution.py:673
  9.1 9.0 %collective-permute-start.1 = (bf16[112,768]{1,0:T(8,128)(2,1)}, bf16[112,768]{1,0:T(8,128)(2,1)S(1)}, u32[]{:S(2)}, u32[]{:S(2)}) collective-permute-start(bf16[112,768]{1,0:T(8,128)(2,1)} %pack.1.refs_0_), channel_id=1, source_target_pairs={{0,2},{1,3},{2,4},{3,5},{4,6},{5,7},{6,0},{7,1},{8,10},{9,11},{10,... | collective-permute-start | bytes 516104 | tf_op jit(solution)/shard_map/ppermute | solution.py:673
  9.2 1.0 %copy-start.1 = (f32[1,2,2,48,512]{4,3,2,1,0:T(8,128)S(1)}, f32[1,2,2,48,512]{4,3,2,1,0:T(8,128)}, u32[]{:S(2)}) copy-start(f32[1,2,2,48,512]{4,3,2,1,0:T(8,128)} %param.6) | copy-start | bytes 1179652
  10.1 0.9 %copy-start.2 = (f32[1,2,48,512]{3,2,1,0:T(8,128)S(1)}, f32[1,2,48,512]{3,2,1,0:T(8,128)}, u32[]{:S(2)}) copy-start(f32[1,2,48,512]{3,2,1,0:T(8,128)} %param.7) | copy-start | bytes 589828
  11.1 0.7 copy-start.3
  11.8 1.0 %copy-start = (bf16[112,768]{1,0:T(8,128)(2,1)S(1)}, bf16[112,768]{1,0:T(8,128)(2,1)}, u32[]{:S(2)}) copy-start(bf16[112,768]{1,0:T(8,128)(2,1)} %pack.1.refs_0_) | copy-start | bytes 516100
  12.8 21.8 %collective-permute-start.5 = (bf16[112,768]{1,0:T(8,128)(2,1)S(1)}, bf16[112,768]{1,0:T(8,128)(2,1)S(1)}, u32[]{:S(2)}, u32[]{:S(2)}) collective-permute-start(bf16[112,768]{1,0:T(8,128)(2,1)S(1)} %copy-done), channel_id=1, source_target_pairs={{0,5},{1,4},{2,7},{3,6},{4,1},{5,0},{6,3},{7,2},{8,13},{9,12},{10,... | collective-permute-start | bytes 516104 | tf_op jit(solution)/shard_map/ppermute | solution.py:673
  13.8 20.8 %collective-permute-start = (bf16[112,768]{1,0:T(8,128)(2,1)S(1)}, bf16[112,768]{1,0:T(8,128)(2,1)S(1)}, u32[]{:S(2)}, u32[]{:S(2)}) collective-permute-start(bf16[112,768]{1,0:T(8,128)(2,1)S(1)} %copy-done), channel_id=1, source_target_pairs={{0,4},{1,5},{2,6},{3,7},{4,0},{5,1},{6,2},{7,3},{8,12},{9,13},{10,... | collective-permute-start | bytes 516104 | tf_op jit(solution)/shard_map/ppermute | solution.py:673
  15.7 18.9 %collective-permute-start.4 = (bf16[112,768]{1,0:T(8,128)(2,1)S(1)}, bf16[112,768]{1,0:T(8,128)(2,1)S(1)}, u32[]{:S(2)}, u32[]{:S(2)}) collective-permute-start(bf16[112,768]{1,0:T(8,128)(2,1)S(1)} %collective-permute-done.3.refs_3_), channel_id=1, source_target_pairs={{0,1},{1,0},{2,3},{3,2},{4,5},{5,4},{6,7},{7,6},{8,9},{9,8},{10,11... | collective-permute-start | bytes 516104 | tf_op jit(solution)/shard_map/ppermute | solution.py:673
  18.1 16.5 %collective-permute-start.2 = (bf16[112,768]{1,0:T(8,128)(2,1)S(1)}, bf16[112,768]{1,0:T(8,128)(2,1)S(1)}, u32[]{:S(2)}, u32[]{:S(2)}) collective-permute-start(bf16[112,768]{1,0:T(8,128)(2,1)S(1)} %collective-permute-done.1.refs_2_), channel_id=1, source_target_pairs={{0,1},{1,0},{2,3},{3,2},{4,5},{5,4},{6,7},{7,6},{8,9},{9,8},{10,11... | collective-permute-start | bytes 516104 | tf_op jit(solution)/shard_map/ppermute | solution.py:673
  18.6 16.0 %copy-start.4 = (f32[1,512]{1,0:T(1,128)S(1)}, f32[1,512]{1,0:T(1,128)}, u32[]{:S(2)}) copy-start(f32[1,512]{1,0:T(1,128)} %refs_8_.1) | copy-start | bytes 6148
  51.3 4.4 %collective-permute-start.7 = (bf16[4,512,512]{2,1,0:T(8,128)(2,1)S(1)}, bf16[4,512,512]{2,1,0:T(8,128)(2,1)}, u32[]{:S(2)}, u32[]{:S(2)}) collective-permute-start(bf16[4,512,512]{2,1,0:T(8,128)(2,1)S(1)} %layer_sum.3.own), channel_id=1, source_target_pairs={{0,8},{8,0},{16,24},{24,16},{1,9},{9,1},{17,25},{25,17},{2,10},{10... | collective-permute-start | bytes 6291464 | tf_op jit(solution)/shard_map/ppermute | solution.py:686
  60.3 8.4 %collective-permute-start.9 = (bf16[2,256,256]{2,1,0:T(8,128)(2,1)S(1)}, bf16[2,256,256]{2,1,0:T(8,128)(2,1)S(1)}, u32[]{:S(2)}, u32[]{:S(2)}) collective-permute-start(bf16[2,256,256]{2,1,0:T(8,128)(2,1)S(1)} %get-tuple-element.19), channel_id=1, source_target_pairs={{0,16},{8,24},{16,0},{24,8},{1,17},{9,25},{17,1},{25,9},{2,18},{10... | collective-permute-start | bytes 786440 | tf_op jit(solution)/shard_map/ppermute | solution.py:695
  61.8 19.3 %collective-permute-start.8 = (bf16[2,512,256]{2,1,0:T(8,128)(2,1)S(1)}, bf16[2,512,256]{2,1,0:T(8,128)(2,1)S(1)}, u32[]{:S(2)}, u32[]{:S(2)}) collective-permute-start(bf16[2,512,256]{2,1,0:T(8,128)(2,1)S(1)} %get-tuple-element.18.after.s_mine), channel_id=1, source_target_pairs={{0,8},{8,0},{16,24},{24,16},{1,9},{9,1},{17,25},{25,17},{2,10},{10... | collective-permute-start | bytes 1572872 | tf_op jit(solution)/shard_map/ppermute | solution.py:695
  68.7 7.6 %collective-permute-start.10 = (bf16[2,256,256]{2,1,0:T(8,128)(2,1)S(1)}, bf16[2,256,256]{2,1,0:T(8,128)(2,1)S(1)}, u32[]{:S(2)}, u32[]{:S(2)}) collective-permute-start(bf16[2,256,256]{2,1,0:T(8,128)(2,1)S(1)} %collective-permute-done.9.q_0), channel_id=1, source_target_pairs={{0,1},{1,0},{2,3},{3,2},{4,5},{5,4},{6,7},{7,6},{8,9},{9,8},{10,11... | collective-permute-start | bytes 786440 | tf_op jit(solution)/shard_map/ppermute | solution.py:673
  70.2 10.9 %collective-permute-start.13 = (bf16[2,832,128]{2,1,0:T(8,128)(2,1)S(1)}, bf16[2,832,128]{2,1,0:T(8,128)(2,1)S(1)}, u32[]{:S(2)}, u32[]{:S(2)}) collective-permute-start(bf16[2,832,128]{2,1,0:T(8,128)(2,1)S(1)} %get-tuple-element.23), channel_id=1, source_target_pairs={{0,16},{8,24},{16,0},{24,8},{1,17},{9,25},{17,1},{25,9},{2,18},{10... | collective-permute-start | bytes 1277960 | tf_op jit(solution)/shard_map/ppermute | solution.py:695
  71.7 9.4 %collective-permute-start.11 = (bf16[2,256,256]{2,1,0:T(8,128)(2,1)S(1)}, bf16[2,256,256]{2,1,0:T(8,128)(2,1)S(1)}, u32[]{:S(2)}, u32[]{:S(2)}) collective-permute-start(bf16[2,256,256]{2,1,0:T(8,128)(2,1)S(1)} %collective-permute-done.9.q_0), channel_id=1, source_target_pairs={{0,8},{8,0},{16,24},{24,16},{1,9},{9,1},{17,25},{25,17},{2,10},{10... | collective-permute-start | bytes 786440 | tf_op jit(solution)/shard_map/ppermute | solution.py:695
  76.3 4.8 %collective-permute-start.12 = (bf16[2,256,256]{2,1,0:T(8,128)(2,1)S(1)}, bf16[2,256,256]{2,1,0:T(8,128)(2,1)S(1)}, u32[]{:S(2)}, u32[]{:S(2)}) collective-permute-start(bf16[2,256,256]{2,1,0:T(8,128)(2,1)S(1)} %collective-permute-done.10.q_1), channel_id=1, source_target_pairs={{0,8},{8,0},{16,24},{24,16},{1,9},{9,1},{17,25},{25,17},{2,10},{10... | collective-permute-start | bytes 786440 | tf_op jit(solution)/shard_map/ppermute | solution.py:695

commit v4 on v3

--- a/solution.py
+++ b/solution.py
@@ -162,10 +162,10 @@
 
 
 def cmul(left, right):
-    return (
-        mm(left[0], right[0]) - mm(left[1], right[1]),
-        mm(left[0], right[1]) + mm(left[1], right[0]),
-    )
+    one = mm(left[0], right[0])
+    two = mm(left[1], right[1])
+    both = mm(left[0] + left[1], right[0] + right[1])
+    return (one - two, both - one - two)
 
 
 def half(pair):

time: 85 us -> 84.2 us (level)
  Pallas kernels: 49.3 us -> 47.8 us
  transfers between devices with their start and end apart: 14 -> 14, of which waited for: 5 -> 5; matrix products, arithmetic and copies ran while one was open for 0% -> 0% of each run, Pallas kernels for 27% -> 26%
where the time goes in v4:
time: 84.2 us; the launch traced here: 84 us
  Pallas kernels  47.8 us (57%)
  waiting for transfers between devices  16.3 us (19%)
  starting transfers between devices  16.2 us (19%)
  local copies, waits for them, and re-layouts  2.7 us (3%)
  between operations  0.95 us (1%)
    pallas_call x2, Pallas kernels, layer_sum(): pl.pallas_call(functools.partial(layer_kernel, count, spheres, multi, las...  32.6 us
    ppermute x8, starting transfers between devices, shifted(): return lax.ppermute(value, 'sph', pairs)  13 us
    ppermute x5, waiting for transfers between devices, crossed(): return lax.ppermute(value, 'layer', [(at, at ^ bit) for at in range(4)])  6.73 us
    ppermute x8, waiting for transfers between devices, shifted(): return lax.ppermute(value, 'sph', pairs)  5.4 us
    pallas_call x1, Pallas kernels, form(): pl.pallas_call(functools.partial(rows_kernel, rows), out_shape=(shape, sh...  4.88 us
    pallas_call x1, Pallas kernels, form(): pl.pallas_call(back_kernel, out_shape=(jax.ShapeDtypeStruct((2, width, wi...  4.28 us
    ppermute x1, waiting for transfers between devices, whole_layers(): other = lax.ppermute(own, 'layer', [(at, at ^ 1) for at in range(4)])  4.16 us
    pallas_call x1, Pallas kernels, join(): pl.pallas_call(functools.partial(join_kernel, rows), out_shape=(shape, sh...  3.1 us
  transfers between devices with their start and end apart: 14, of which 5 were waited for; matrix products, arithmetic and copies ran while one was open for 0% of the time, Pallas kernels for 26%

profile of v4, /device:TPU:0, one launch (start us, length us, event | category | flops | bytes accessed | tf_op | source)
XLA Modules:
  0.0 84.0 jit_solution(1529953155521569819)
XLA Ops:
  0.6 1.9 %pack.1.refs_0_ = bf16[112,768]{1,0:T(8,128)(2,1)} custom-call(f32[16,2,48,48]{3,2,1,0:T(8,128)} %bitcast.10, s32[1,16]{1,0:T(1,128)} %sites.1), custom_call_target="tpu_custom_call" | custom-call | tf_op jit(solution)/shard_map/pack/pallas_call | solution.py:385
  2.6 3.0 %collective-permute-start.6 = (bf16[112,768]{1,0:T(8,128)(2,1)}, bf16[112,768]{1,0:T(8,128)(2,1)S(1)}, u32[]{:S(2)}, u32[]{:S(2)}) collective-permute-start(bf16[112,768]{1,0:T(8,128)(2,1)} %pack.1.refs_0_), channel_id=1, source_target_pairs={{0,1},{1,0},{2,3},{3,2},{4,5},{5,4},{6,7},{7,6},{8,9},{9,8},{10,11... | collective-permute-start | bytes 516104 | tf_op jit(solution)/shard_map/ppermute | solution.py:673
  5.5 3.6 %collective-permute-start.3 = (bf16[112,768]{1,0:T(8,128)(2,1)}, bf16[112,768]{1,0:T(8,128)(2,1)S(1)}, u32[]{:S(2)}, u32[]{:S(2)}) collective-permute-start(bf16[112,768]{1,0:T(8,128)(2,1)} %pack.1.refs_0_), channel_id=1, source_target_pairs={{0,6},{1,7},{2,0},{3,1},{4,2},{5,3},{6,4},{7,5},{8,14},{9,15},{10,... | collective-permute-start | bytes 516104 | tf_op jit(solution)/shard_map/ppermute | solution.py:673
  9.1 0.0 collective-permute-start.1
  9.2 1.0 %copy-done.1 = f32[1,2,2,48,512]{4,3,2,1,0:T(8,128)S(1)} copy-done((f32[1,2,2,48,512]{4,3,2,1,0:T(8,128)S(1)}, f32[1,2,2,48,512]{4,3,2,1,0:T(8,128)}, u32[]{:S(2)}) %copy-start.1) | copy-done | bytes 393240
  10.2 0.9 %copy-done.2 = f32[1,2,48,512]{3,2,1,0:T(8,128)S(1)} copy-done((f32[1,2,48,512]{3,2,1,0:T(8,128)S(1)}, f32[1,2,48,512]{3,2,1,0:T(8,128)}, u32[]{:S(2)}) %copy-start.2) | copy-done | bytes 196632
  11.1 0.7 copy-done.3
  11.8 1.0 %prepare.1 = (bf16[2,1024,768]{2,1,0:T(8,128)(2,1)S(1)}, bf16[96,1024]{1,0:T(8,128)(2,1)S(1)}, bf16[16,256]{1,0:T(8,128)(2,1)S(1)}) custom-call(f32[2,2,48,512]{3,2,1,0:T(8,128)S(1)} %bitcast.8, f32[2,48,512]{2,1,0:T(8,128)S(1)} %bitcast.9, s32[2,256]{1,0:T(2,128)S(1)} %copy-done.3), custom_call_target="tpu_custom_call" | custom-call | flops 2147483648 | bytes 4194304 | tf_op jit(solution)/shard_map/prepare/pallas_call | solution.py:416
  12.8 1.0 %collective-permute-start.5 = (bf16[112,768]{1,0:T(8,128)(2,1)S(1)}, bf16[112,768]{1,0:T(8,128)(2,1)S(1)}, u32[]{:S(2)}, u32[]{:S(2)}) collective-permute-start(bf16[112,768]{1,0:T(8,128)(2,1)S(1)} %copy-done), channel_id=1, source_target_pairs={{0,5},{1,4},{2,7},{3,6},{4,1},{5,0},{6,3},{7,2},{8,13},{9,12},{10,... | collective-permute-start | bytes 516104 | tf_op jit(solution)/shard_map/ppermute | solution.py:673
  13.8 1.9 %collective-permute-start = (bf16[112,768]{1,0:T(8,128)(2,1)S(1)}, bf16[112,768]{1,0:T(8,128)(2,1)S(1)}, u32[]{:S(2)}, u32[]{:S(2)}) collective-permute-start(bf16[112,768]{1,0:T(8,128)(2,1)S(1)} %copy-done), channel_id=1, source_target_pairs={{0,4},{1,5},{2,6},{3,7},{4,0},{5,1},{6,2},{7,3},{8,12},{9,13},{10,... | collective-permute-start | bytes 516104 | tf_op jit(solution)/shard_map/ppermute | solution.py:673
  15.7 0.0 collective-permute-done.3.refs_3_
  15.7 1.5 %collective-permute-start.4 = (bf16[112,768]{1,0:T(8,128)(2,1)S(1)}, bf16[112,768]{1,0:T(8,128)(2,1)S(1)}, u32[]{:S(2)}, u32[]{:S(2)}) collective-permute-start(bf16[112,768]{1,0:T(8,128)(2,1)S(1)} %collective-permute-done.3.refs_3_), channel_id=1, source_target_pairs={{0,1},{1,0},{2,3},{3,2},{4,5},{5,4},{6,7},{7,6},{8,9},{9,8},{10,11... | collective-permute-start | bytes 516104 | tf_op jit(solution)/shard_map/ppermute | solution.py:673
  17.2 0.9 %collective-permute-done.1.refs_2_ = bf16[112,768]{1,0:T(8,128)(2,1)S(1)} collective-permute-done((bf16[112,768]{1,0:T(8,128)(2,1)}, bf16[112,768]{1,0:T(8,128)(2,1)S(1)}, u32[]{:S(2)}, u32[]{:S(2)}) %collective-permute-start.1) | collective-permute-done | bytes 172064 | tf_op jit(solution)/shard_map/ppermute | solution.py:673
  18.1 0.5 collective-permute-start.2
  18.6 16.0 %layer_sum.2.refs_7_ = f32[2,1024,512]{2,1,0:T(8,128)S(1)} custom-call(bf16[112,768]{1,0:T(8,128)(2,1)S(1)} %copy-done, bf16[112,768]{1,0:T(8,128)(2,1)S(1)} %collective-permute-done.6.refs_1_, bf16[112,768]{1,0:T(8,128)(2,1)S(1)} %collective-permute-done.1.refs_2_, bf16[112,768]{1,0:T(8,128)(2,1)S(1)} %collective-permute-done.3.refs_3_, ...), custom_call_target="tpu_custom_call" | custom-call | flops 9663676416 | bytes 8388608 | tf_op jit(solution)/shard_map/layer_sum/pallas_call | solution.py:456
  34.6 0.0 collective-permute-done.4.refs_2_
  34.7 16.7 %layer_sum.3.own = bf16[4,512,512]{2,1,0:T(8,128)(2,1)S(1)} custom-call(bf16[112,768]{1,0:T(8,128)(2,1)S(1)} %collective-permute-done.refs_0_, bf16[112,768]{1,0:T(8,128)(2,1)S(1)} %collective-permute-done.2.refs_1_, bf16[112,768]{1,0:T(8,128)(2,1)S(1)} %collective-permute-done.4.refs_2_, bf16[112,768]{1,0:T(8,128)(2,1)S(1)} %collective-permute-done.5.refs_3_, ...), custom_call_target="tpu_custom_call" | custom-call | flops 9663676416 | bytes 8388608 | tf_op jit(solution)/shard_map/layer_sum/pallas_call | solution.py:456
  51.3 0.1 collective-permute-start.7
  51.5 0.1 stack.23.place
  51.5 4.2 %collective-permute-done.7.other = bf16[4,512,512]{2,1,0:T(8,128)(2,1)} collective-permute-done((bf16[4,512,512]{2,1,0:T(8,128)(2,1)S(1)}, bf16[4,512,512]{2,1,0:T(8,128)(2,1)}, u32[]{:S(2)}, u32[]{:S(2)}) %collective-permute-start.7) | collective-permute-done | bytes 2097184 | tf_op jit(solution)/shard_map/ppermute | solution.py:686
  55.7 4.3 %back.1 = (bf16[2,512,256]{2,1,0:T(8,128)(2,1)S(1)}, bf16[2,256,256]{2,1,0:T(8,128)(2,1)S(1)}) custom-call(s32[5]{0:T(128)S(1)} %stack.23.place, bf16[4,512,512]{2,1,0:T(8,128)(2,1)S(1)} %layer_sum.3.own, bf16[4,512,512]{2,1,0:T(8,128)(2,1)} %collective-permute-done.7.other), custom_call_target="tpu_custom_call" | custom-call | flops 4294967296 | bytes 8388608 | tf_op jit(solution)/shard_map/back/pallas_call | solution.py:552
  60.0 1.5 %collective-permute-start.9 = (bf16[2,256,256]{2,1,0:T(8,128)(2,1)S(1)}, bf16[2,256,256]{2,1,0:T(8,128)(2,1)S(1)}, u32[]{:S(2)}, u32[]{:S(2)}) collective-permute-start(bf16[2,256,256]{2,1,0:T(8,128)(2,1)S(1)} %get-tuple-element.19), channel_id=1, source_target_pairs={{0,16},{8,24},{16,0},{24,8},{1,17},{9,25},{17,1},{25,9},{2,18},{10... | collective-permute-start | bytes 786440 | tf_op jit(solution)/shard_map/ppermute | solution.py:695
  61.5 0.0 collective-permute-start.8
  61.5 4.9 %rows.1 = (bf16[2,832,128]{2,1,0:T(8,128)(2,1)S(1)}, bf16[2,832,128]{2,1,0:T(8,128)(2,1)S(1)}) custom-call(s32[5]{0:T(128)S(1)} %stack.23.place, bf16[4,512,512]{2,1,0:T(8,128)(2,1)S(1)} %layer_sum.3.own, bf16[4,512,512]{2,1,0:T(8,128)(2,1)} %collective-permute-done.7.other, bf16[2,512,256]{2,1,0:T(8,128)(2,1)S(1)} %get-tuple-element.18.after.s_mine), custom_call_target="tpu_custom_call" | custom-call | flops 4294967296 | bytes 8388608 | tf_op jit(solution)/shard_map/rows/pallas_call | solution.py:566
  66.4 2.0 %collective-permute-done.9.q_0 = bf16[2,256,256]{2,1,0:T(8,128)(2,1)S(1)} collective-permute-done((bf16[2,256,256]{2,1,0:T(8,128)(2,1)S(1)}, bf16[2,256,256]{2,1,0:T(8,128)(2,1)S(1)}, u32[]{:S(2)}, u32[]{:S(2)}) %collective-permute-start.9) | collective-permute-done | bytes 262176 | tf_op jit(solution)/shard_map/ppermute | solution.py:695
  68.4 1.5 %collective-permute-start.10 = (bf16[2,256,256]{2,1,0:T(8,128)(2,1)S(1)}, bf16[2,256,256]{2,1,0:T(8,128)(2,1)S(1)}, u32[]{:S(2)}, u32[]{:S(2)}) collective-permute-start(bf16[2,256,256]{2,1,0:T(8,128)(2,1)S(1)} %collective-permute-done.9.q_0), channel_id=1, source_target_pairs={{0,1},{1,0},{2,3},{3,2},{4,5},{5,4},{6,7},{7,6},{8,9},{9,8},{10,11... | collective-permute-start | bytes 786440 | tf_op jit(solution)/shard_map/ppermute | solution.py:673
  69.9 1.5 %collective-permute-start.13 = (bf16[2,832,128]{2,1,0:T(8,128)(2,1)S(1)}, bf16[2,832,128]{2,1,0:T(8,128)(2,1)S(1)}, u32[]{:S(2)}, u32[]{:S(2)}) collective-permute-start(bf16[2,832,128]{2,1,0:T(8,128)(2,1)S(1)} %get-tuple-element.23), channel_id=1, source_target_pairs={{0,16},{8,24},{16,0},{24,8},{1,17},{9,25},{17,1},{25,9},{2,18},{10... | collective-permute-start | bytes 1277960 | tf_op jit(solution)/shard_map/ppermute | solution.py:695
  71.4 0.0 collective-permute-start.11
  71.4 4.5 %collective-permute-done.10.q_1 = bf16[2,256,256]{2,1,0:T(8,128)(2,1)S(1)} collective-permute-done((bf16[2,256,256]{2,1,0:T(8,128)(2,1)S(1)}, bf16[2,256,256]{2,1,0:T(8,128)(2,1)S(1)}, u32[]{:S(2)}, u32[]{:S(2)}) %collective-permute-start.10) | collective-permute-done | bytes 262176 | tf_op jit(solution)/shard_map/ppermute | solution.py:673
  75.9 4.7 %collective-permute-done.13.h_sent = bf16[2,832,128]{2,1,0:T(8,128)(2,1)S(1)} collective-permute-done((bf16[2,832,128]{2,1,0:T(8,128)(2,1)S(1)}, bf16[2,832,128]{2,1,0:T(8,128)(2,1)S(1)}, u32[]{:S(2)}, u32[]{:S(2)}) %collective-permute-start.13) | collective-permute-done | bytes 426016 | tf_op jit(solution)/shard_map/ppermute | solution.py:695
  80.7 0.0 collective-permute-done.12.q_3
  80.7 3.1 %join.1 = (f32[2,64,128]{2,1,0:T(8,128)}, f32[2,64,128]{2,1,0:T(8,128)}) custom-call(s32[5]{0:T(128)S(1)} %stack.23.place, bf16[2,512,256]{2,1,0:T(8,128)(2,1)S(1)} %get-tuple-element.18.after.s_mine, bf16[2,512,256]{2,1,0:T(8,128)(2,1)S(1)} %collective-permute-done.8.s_side, bf16[2,256,256]{2,1,0:T(8,128)(2,1)S(1)} %collective-permute-done.9.q_0, ...), custom_call_target="tpu_custom_call" | custom-call | flops 1073741824 | bytes 4194304 | tf_op jit(solution)/shard_map/join/pallas_call | solution.py:641
  (14 shorter events, 0.0 us)
Async XLA Ops:
  2.6 16.1 %collective-permute-start.6 = (bf16[112,768]{1,0:T(8,128)(2,1)}, bf16[112,768]{1,0:T(8,128)(2,1)S(1)}, u32[]{:S(2)}, u32[]{:S(2)}) collective-permute-start(bf16[112,768]{1,0:T(8,128)(2,1)} %pack.1.refs_0_), channel_id=1, source_target_pairs={{0,1},{1,0},{2,3},{3,2},{4,5},{5,4},{6,7},{7,6},{8,9},{9,8},{10,11... | collective-permute-start | bytes 516104 | tf_op jit(solution)/shard_map/ppermute | solution.py:673
  5.5 10.2 %collective-permute-start.3 = (bf16[112,768]{1,0:T(8,128)(2,1)}, bf16[112,768]{1,0:T(8,128)(2,1)S(1)}, u32[]{:S(2)}, u32[]{:S(2)}) collective-permute-start(bf16[112,768]{1,0:T(8,128)(2,1)} %pack.1.refs_0_), channel_id=1, source_target_pairs={{0,6},{1,7},{2,0},{3,1},{4,2},{5,3},{6,4},{7,5},{8,14},{9,15},{10,... | collective-permute-start | bytes 516104 | tf_op jit(solution)/shard_map/ppermute | solution.py:673
  9.1 9.0 %collective-permute-start.1 = (bf16[112,768]{1,0:T(8,128)(2,1)}, bf16[112,768]{1,0:T(8,128)(2,1)S(1)}, u32[]{:S(2)}, u32[]{:S(2)}) collective-permute-start(bf16[112,768]{1,0:T(8,128)(2,1)} %pack.1.refs_0_), channel_id=1, source_target_pairs={{0,2},{1,3},{2,4},{3,5},{4,6},{5,7},{6,0},{7,1},{8,10},{9,11},{10,... | collective-permute-start | bytes 516104 | tf_op jit(solution)/shard_map/ppermute | solution.py:673
  9.2 1.0 %copy-start.1 = (f32[1,2,2,48,512]{4,3,2,1,0:T(8,128)S(1)}, f32[1,2,2,48,512]{4,3,2,1,0:T(8,128)}, u32[]{:S(2)}) copy-start(f32[1,2,2,48,512]{4,3,2,1,0:T(8,128)} %param.6) | copy-start | bytes 1179652
  10.1 0.9 %copy-start.2 = (f32[1,2,48,512]{3,2,1,0:T(8,128)S(1)}, f32[1,2,48,512]{3,2,1,0:T(8,128)}, u32[]{:S(2)}) copy-start(f32[1,2,48,512]{3,2,1,0:T(8,128)} %param.7) | copy-start | bytes 589828
  11.1 0.7 copy-start.3
  11.8 1.0 %copy-start = (bf16[112,768]{1,0:T(8,128)(2,1)S(1)}, bf16[112,768]{1,0:T(8,128)(2,1)}, u32[]{:S(2)}) copy-start(bf16[112,768]{1,0:T(8,128)(2,1)} %pack.1.refs_0_) | copy-start | bytes 516100
  12.8 21.8 %collective-permute-start.5 = (bf16[112,768]{1,0:T(8,128)(2,1)S(1)}, bf16[112,768]{1,0:T(8,128)(2,1)S(1)}, u32[]{:S(2)}, u32[]{:S(2)}) collective-permute-start(bf16[112,768]{1,0:T(8,128)(2,1)S(1)} %copy-done), channel_id=1, source_target_pairs={{0,5},{1,4},{2,7},{3,6},{4,1},{5,0},{6,3},{7,2},{8,13},{9,12},{10,... | collective-permute-start | bytes 516104 | tf_op jit(solution)/shard_map/ppermute | solution.py:673
  13.8 20.8 %collective-permute-start = (bf16[112,768]{1,0:T(8,128)(2,1)S(1)}, bf16[112,768]{1,0:T(8,128)(2,1)S(1)}, u32[]{:S(2)}, u32[]{:S(2)}) collective-permute-start(bf16[112,768]{1,0:T(8,128)(2,1)S(1)} %copy-done), channel_id=1, source_target_pairs={{0,4},{1,5},{2,6},{3,7},{4,0},{5,1},{6,2},{7,3},{8,12},{9,13},{10,... | collective-permute-start | bytes 516104 | tf_op jit(solution)/shard_map/ppermute | solution.py:673
  15.7 18.9 %collective-permute-start.4 = (bf16[112,768]{1,0:T(8,128)(2,1)S(1)}, bf16[112,768]{1,0:T(8,128)(2,1)S(1)}, u32[]{:S(2)}, u32[]{:S(2)}) collective-permute-start(bf16[112,768]{1,0:T(8,128)(2,1)S(1)} %collective-permute-done.3.refs_3_), channel_id=1, source_target_pairs={{0,1},{1,0},{2,3},{3,2},{4,5},{5,4},{6,7},{7,6},{8,9},{9,8},{10,11... | collective-permute-start | bytes 516104 | tf_op jit(solution)/shard_map/ppermute | solution.py:673
  18.1 16.5 %collective-permute-start.2 = (bf16[112,768]{1,0:T(8,128)(2,1)S(1)}, bf16[112,768]{1,0:T(8,128)(2,1)S(1)}, u32[]{:S(2)}, u32[]{:S(2)}) collective-permute-start(bf16[112,768]{1,0:T(8,128)(2,1)S(1)} %collective-permute-done.1.refs_2_), channel_id=1, source_target_pairs={{0,1},{1,0},{2,3},{3,2},{4,5},{5,4},{6,7},{7,6},{8,9},{9,8},{10,11... | collective-permute-start | bytes 516104 | tf_op jit(solution)/shard_map/ppermute | solution.py:673
  18.6 16.0 %copy-start.4 = (f32[1,512]{1,0:T(1,128)S(1)}, f32[1,512]{1,0:T(1,128)}, u32[]{:S(2)}) copy-start(f32[1,512]{1,0:T(1,128)} %refs_8_.1) | copy-start | bytes 6148
  51.3 4.4 %collective-permute-start.7 = (bf16[4,512,512]{2,1,0:T(8,128)(2,1)S(1)}, bf16[4,512,512]{2,1,0:T(8,128)(2,1)}, u32[]{:S(2)}, u32[]{:S(2)}) collective-permute-start(bf16[4,512,512]{2,1,0:T(8,128)(2,1)S(1)} %layer_sum.3.own), channel_id=1, source_target_pairs={{0,8},{8,0},{16,24},{24,16},{1,9},{9,1},{17,25},{25,17},{2,10},{10... | collective-permute-start | bytes 6291464 | tf_op jit(solution)/shard_map/ppermute | solution.py:686
  60.0 8.4 %collective-permute-start.9 = (bf16[2,256,256]{2,1,0:T(8,128)(2,1)S(1)}, bf16[2,256,256]{2,1,0:T(8,128)(2,1)S(1)}, u32[]{:S(2)}, u32[]{:S(2)}) collective-permute-start(bf16[2,256,256]{2,1,0:T(8,128)(2,1)S(1)} %get-tuple-element.19), channel_id=1, source_target_pairs={{0,16},{8,24},{16,0},{24,8},{1,17},{9,25},{17,1},{25,9},{2,18},{10... | collective-permute-start | bytes 786440 | tf_op jit(solution)/shard_map/ppermute | solution.py:695
  61.5 19.1 %collective-permute-start.8 = (bf16[2,512,256]{2,1,0:T(8,128)(2,1)S(1)}, bf16[2,512,256]{2,1,0:T(8,128)(2,1)S(1)}, u32[]{:S(2)}, u32[]{:S(2)}) collective-permute-start(bf16[2,512,256]{2,1,0:T(8,128)(2,1)S(1)} %get-tuple-element.18.after.s_mine), channel_id=1, source_target_pairs={{0,8},{8,0},{16,24},{24,16},{1,9},{9,1},{17,25},{25,17},{2,10},{10... | collective-permute-start | bytes 1572872 | tf_op jit(solution)/shard_map/ppermute | solution.py:695
  68.4 7.5 %collective-permute-start.10 = (bf16[2,256,256]{2,1,0:T(8,128)(2,1)S(1)}, bf16[2,256,256]{2,1,0:T(8,128)(2,1)S(1)}, u32[]{:S(2)}, u32[]{:S(2)}) collective-permute-start(bf16[2,256,256]{2,1,0:T(8,128)(2,1)S(1)} %collective-permute-done.9.q_0), channel_id=1, source_target_pairs={{0,1},{1,0},{2,3},{3,2},{4,5},{5,4},{6,7},{7,6},{8,9},{9,8},{10,11... | collective-permute-start | bytes 786440 | tf_op jit(solution)/shard_map/ppermute | solution.py:673
  69.9 10.8 %collective-permute-start.13 = (bf16[2,832,128]{2,1,0:T(8,128)(2,1)S(1)}, bf16[2,832,128]{2,1,0:T(8,128)(2,1)S(1)}, u32[]{:S(2)}, u32[]{:S(2)}) collective-permute-start(bf16[2,832,128]{2,1,0:T(8,128)(2,1)S(1)} %get-tuple-element.23), channel_id=1, source_target_pairs={{0,16},{8,24},{16,0},{24,8},{1,17},{9,25},{17,1},{25,9},{2,18},{10... | collective-permute-start | bytes 1277960 | tf_op jit(solution)/shard_map/ppermute | solution.py:695
  71.4 9.3 %collective-permute-start.11 = (bf16[2,256,256]{2,1,0:T(8,128)(2,1)S(1)}, bf16[2,256,256]{2,1,0:T(8,128)(2,1)S(1)}, u32[]{:S(2)}, u32[]{:S(2)}) collective-permute-start(bf16[2,256,256]{2,1,0:T(8,128)(2,1)S(1)} %collective-permute-done.9.q_0), channel_id=1, source_target_pairs={{0,8},{8,0},{16,24},{24,16},{1,9},{9,1},{17,25},{25,17},{2,10},{10... | collective-permute-start | bytes 786440 | tf_op jit(solution)/shard_map/ppermute | solution.py:695
  75.9 4.8 %collective-permute-start.12 = (bf16[2,256,256]{2,1,0:T(8,128)(2,1)S(1)}, bf16[2,256,256]{2,1,0:T(8,128)(2,1)S(1)}, u32[]{:S(2)}, u32[]{:S(2)}) collective-permute-start(bf16[2,256,256]{2,1,0:T(8,128)(2,1)S(1)} %collective-permute-done.10.q_1), channel_id=1, source_target_pairs={{0,8},{8,0},{16,24},{24,16},{1,9},{9,1},{17,25},{25,17},{2,10},{10... | collective-permute-start | bytes 786440 | tf_op jit(solution)/shard_map/ppermute | solution.py:695
